TPU v7x, 32 devices: a whole 2x2x4 slice. The times are simulated.
32 devices in a mesh: section: 2 (over x), ctx: 2 (over y), shard: 8 (over z, core).
Axes of the slice: x: 2, y: 2, z: 4, core: 2. Of those that a mesh axis runs over, the one named last changes fastest.
Arguments:
- inputs: bfloat16 [2, 8, 1024, 576], P(None, 'shard', 'ctx'), may hold values from -6 to 6
- cotangent: bfloat16 [2, 8, 1024, 576], P(None, 'shard', 'ctx'), may hold values from -6 to 6
- attn_gain: bfloat16 [2, 576], P('section', 'shard'), may hold values from 0.5 to 1.5
- w_query: bfloat16 [2, 576, 576], P('section', 'shard'), may hold values from -0.25 to 0.25
- w_key: bfloat16 [2, 576, 192], P('section', 'shard'), may hold values from -0.25 to 0.25
- w_value: bfloat16 [2, 576, 192], P('section', 'shard'), may hold values from -0.25 to 0.25
- w_out: bfloat16 [2, 576, 576], P('section', 'shard'), may hold values from -3 to 3
- mlp_gain: bfloat16 [2, 576], P('section', 'shard'), may hold values from 0.5 to 1.5
- w_gate: bfloat16 [2, 576, 1536], P('section', 'shard'), may hold values from -0.25 to 0.25
- w_up: bfloat16 [2, 576, 1536], P('section', 'shard'), may hold values from -0.25 to 0.25
- w_down: bfloat16 [2, 1536, 576], P('section', 'shard'), may hold values from -0.15625 to 0.15625
Outputs:
- activations: bfloat16 [2, 2, 8, 1024, 576], P('section', None, 'shard', 'ctx')
- input_grads: bfloat16 [2, 2, 8, 1024, 576], P('section', None, 'shard', 'ctx')
- grad_attn_gain: float32 [2, 576], P('section', 'shard')
- grad_query: float32 [2, 576, 576], P('section', 'shard')
- grad_key: float32 [2, 576, 192], P('section', 'shard')
- grad_value: float32 [2, 576, 192], P('section', 'shard')
- grad_out: float32 [2, 576, 576], P('section', 'shard')
- grad_mlp_gain: float32 [2, 576], P('section', 'shard')
- grad_gate: float32 [2, 576, 1536], P('section', 'shard')
- grad_up: float32 [2, 576, 1536], P('section', 'shard')
- grad_down: float32 [2, 1536, 576], P('section', 'shard')
All inputs are finite; a program needn't handle non-finite values.
Results may differ from a plain program's by a relative error of at most 0.025.
Values may be sent and summed in bfloat16 or wider, within the bound.
A program may use at most 256 MiB of HBM per device.

v0:
```python
import jax
import jax.numpy as jnp
from jax import lax
from jax.sharding import PartitionSpec as P

HEADS = 9
KV_HEADS = 3
HEAD_DIM = 64


epsilon = 1e-05
rope_base = 100000.0


def shifted(x, axis, by):
    devices = lax.axis_size(axis)
    pairs = [(i, i + by) for i in range(devices) if 0 <= i + by < devices]
    return lax.ppermute(x, axis, pairs)


def rope_tables(positions):
    half_dim = HEAD_DIM // 2
    frequency = rope_base ** (-(jnp.arange(half_dim).astype(jnp.float32) * 2.0 / HEAD_DIM))
    angles = positions.astype(jnp.float32)[:, None] * frequency[None, :]
    cosine = jnp.cos(angles)
    sine_table = jnp.sin(angles)
    return (jnp.concatenate([cosine, cosine], -1), jnp.concatenate([sine_table, sine_table], -1))


def rotate(source, cosine, sine_table):
    half_dim = source.shape[-1] // 2
    turned = jnp.concatenate([-source[..., half_dim:], source[..., :half_dim]], -1)
    return source * cosine[:, None, :] + turned * sine_table[:, None, :]


def norm_forward(source, gain_vec):
    return source * lax.rsqrt(jnp.mean(source * source, -1, keepdims=True) + epsilon) * gain_vec


def norm_back(source, gain_vec, grad_normed, grad_carry):
    factor = lax.rsqrt(jnp.mean(source * source, -1, keepdims=True) + epsilon)
    unit_rows = source * factor
    gain_grad = jnp.sum(grad_normed * unit_rows, axis=(0, 1))
    scaled = grad_normed * gain_vec
    return (
        grad_carry
        + factor * (scaled - unit_rows * jnp.mean(scaled * unit_rows, -1, keepdims=True)),
        gain_grad,
    )


def attention_scores(queries, keys_all, block_pos):
    seq_rows = queries.shape[1]
    full_len = keys_all.shape[1]
    scores = jnp.einsum(
        "sqkgd,sjkd->skgqj", queries, keys_all, preferred_element_type=jnp.float32
    ) * HEAD_DIM ** (-0.5)
    query_places = block_pos * seq_rows + jnp.arange(seq_rows)
    causal = jnp.arange(full_len)[None, :] <= query_places[:, None]
    return jnp.where(causal, scores, -1e30)


def forward_layer(layer_in, weights, block_pos, cosine, sine_table):
    gain_attn, query_w, key_w, value_w, out_w, gain_mlp, gate_w, up_w, down_w = weights
    seq_count, seq_rows, model_width = layer_in.shape
    groups = HEADS // KV_HEADS
    hidden_in = layer_in.astype(jnp.float32)
    normed = norm_forward(hidden_in, gain_attn).astype(jnp.bfloat16)
    query_raw = jnp.dot(normed, query_w, preferred_element_type=jnp.float32).reshape(
        seq_count, seq_rows, HEADS, HEAD_DIM
    )
    key_raw = jnp.dot(normed, key_w, preferred_element_type=jnp.float32).reshape(
        seq_count, seq_rows, KV_HEADS, HEAD_DIM
    )
    queries = (
        rotate(query_raw, cosine, sine_table)
        .astype(jnp.bfloat16)
        .reshape(seq_count, seq_rows, KV_HEADS, groups, HEAD_DIM)
    )
    key_rows = (
        rotate(key_raw, cosine, sine_table)
        .astype(jnp.bfloat16)
        .reshape(seq_count, seq_rows, KV_HEADS * HEAD_DIM)
    )
    values = jnp.dot(normed, value_w, preferred_element_type=jnp.float32).astype(jnp.bfloat16)
    keys_flat, values_flat = (
        lax.all_gather(key_rows, "ctx", axis=1, tiled=True),
        lax.all_gather(values, "ctx", axis=1, tiled=True),
    )
    full_len = keys_flat.shape[1]
    keys_all = keys_flat.reshape(seq_count, full_len, KV_HEADS, HEAD_DIM)
    values_all = values_flat.reshape(seq_count, full_len, KV_HEADS, HEAD_DIM)
    scores = attention_scores(queries, keys_all, block_pos)
    row_max = jnp.max(scores, -1, keepdims=True)
    exp_terms = jnp.exp(scores - row_max)
    row_total = jnp.sum(exp_terms, -1, keepdims=True)
    log_total = row_max + jnp.log(row_total)
    attn_probs = (exp_terms / row_total).astype(jnp.bfloat16)
    attn_mixed = jnp.einsum(
        "skgqj,sjkd->sqkgd", attn_probs, values_all, preferred_element_type=jnp.float32
    )
    attn_mixed = attn_mixed.reshape(seq_count, seq_rows, HEADS * HEAD_DIM).astype(jnp.bfloat16)
    residual = hidden_in + jnp.dot(attn_mixed, out_w, preferred_element_type=jnp.float32)
    normed_mlp = norm_forward(residual, gain_mlp).astype(jnp.bfloat16)
    gate_pre = jnp.dot(normed_mlp, gate_w, preferred_element_type=jnp.float32)
    up_proj = jnp.dot(normed_mlp, up_w, preferred_element_type=jnp.float32)
    hidden = (gate_pre * jax.nn.sigmoid(gate_pre) * up_proj).astype(jnp.bfloat16)
    layer_out = residual + jnp.dot(hidden, down_w, preferred_element_type=jnp.float32)
    stored = (
        layer_in,
        normed,
        queries,
        keys_all,
        values_all,
        log_total,
        attn_mixed,
        residual,
        normed_mlp,
        gate_pre,
        up_proj,
        hidden,
    )
    return (layer_out.astype(jnp.bfloat16), stored)


def weight_grads(factors, gain_grads):
    (
        hidden,
        grad_out,
        normed_mlp,
        grad_gate,
        grad_up,
        attn_mixed,
        grad_attn,
        normed,
        grad_queries,
        grad_keys,
        grad_values,
    ) = factors

    def product(left, right):
        return jnp.einsum("srd,sri->di", left, right, preferred_element_type=jnp.float32)

    return (
        gain_grads[0],
        product(normed, grad_queries),
        product(normed, grad_keys),
        product(normed, grad_values),
        product(attn_mixed, grad_attn),
        gain_grads[1],
        product(normed_mlp, grad_gate),
        product(normed_mlp, grad_up),
        product(hidden, grad_out),
    )


def backward_layer(grad_out, stored, weights, block_pos, cosine, sine_table):
    gain_attn, query_w, key_w, value_w, out_w, gain_mlp, gate_w, up_w, down_w = weights
    (
        layer_in,
        normed,
        queries,
        keys_all,
        values_all,
        log_total,
        attn_mixed,
        residual,
        normed_mlp,
        gate_pre,
        up_proj,
        hidden,
    ) = stored
    seq_count, seq_rows = (layer_in.shape[0], layer_in.shape[1])
    full_len = keys_all.shape[1]
    score_scale = HEAD_DIM ** (-0.5)
    grad_resid = grad_out.astype(jnp.float32)
    grad_hidden = jnp.einsum("srd,id->sri", grad_out, down_w, preferred_element_type=jnp.float32)
    sigmoid_gate = jax.nn.sigmoid(gate_pre)
    grad_gate = (
        grad_hidden * up_proj * sigmoid_gate * (1.0 + gate_pre * (1.0 - sigmoid_gate))
    ).astype(jnp.bfloat16)
    grad_up = (grad_hidden * gate_pre * sigmoid_gate).astype(jnp.bfloat16)
    grad_normed = jnp.einsum(
        "srf,df->srd", grad_gate, gate_w, preferred_element_type=jnp.float32
    ) + jnp.einsum("srf,df->srd", grad_up, up_w, preferred_element_type=jnp.float32)
    grad_resid, g_gain_mlp = norm_back(residual, gain_mlp, grad_normed, grad_resid)
    grad_attn = grad_resid.astype(jnp.bfloat16)
    grad_mixed = jnp.einsum(
        "srd,id->sri", grad_attn, out_w, preferred_element_type=jnp.float32
    ).astype(jnp.bfloat16)
    grad_mixed = grad_mixed.reshape(seq_count, seq_rows, KV_HEADS, HEADS // KV_HEADS, HEAD_DIM)
    scores = attention_scores(queries, keys_all, block_pos)
    attn_probs = jnp.exp(scores - log_total)
    grad_probs = jnp.einsum(
        "sqkgd,sjkd->skgqj", grad_mixed, values_all, preferred_element_type=jnp.float32
    )
    grad_scores = (
        attn_probs * (grad_probs - jnp.sum(attn_probs * grad_probs, -1, keepdims=True))
    ).astype(jnp.bfloat16)
    grad_queries = (
        jnp.einsum("skgqj,sjkd->sqkgd", grad_scores, keys_all, preferred_element_type=jnp.float32)
        * score_scale
    )
    grad_queries = rotate(
        grad_queries.reshape(seq_count, seq_rows, HEADS, HEAD_DIM), cosine, -sine_table
    )
    grad_queries = grad_queries.reshape(seq_count, seq_rows, HEADS * HEAD_DIM).astype(jnp.bfloat16)
    key_terms = (
        jnp.einsum("skgqj,sqkgd->sjkd", grad_scores, queries, preferred_element_type=jnp.float32)
        * score_scale
    )
    value_terms = jnp.einsum(
        "skgqj,sqkgd->sjkd",
        attn_probs.astype(jnp.bfloat16),
        grad_mixed,
        preferred_element_type=jnp.float32,
    )
    key_part, value_part = (
        lax.psum_scatter(
            key_terms.reshape(seq_count, full_len, KV_HEADS * HEAD_DIM).astype(jnp.bfloat16),
            "ctx",
            scatter_dimension=1,
            tiled=True,
        ).astype(jnp.float32),
        lax.psum_scatter(
            value_terms.reshape(seq_count, full_len, KV_HEADS * HEAD_DIM).astype(jnp.bfloat16),
            "ctx",
            scatter_dimension=1,
            tiled=True,
        ).astype(jnp.float32),
    )
    grad_keys = rotate(
        key_part.reshape(seq_count, seq_rows, KV_HEADS, HEAD_DIM), cosine, -sine_table
    )
    grad_keys = grad_keys.reshape(seq_count, seq_rows, KV_HEADS * HEAD_DIM).astype(jnp.bfloat16)
    grad_values = value_part.astype(jnp.bfloat16)
    grad_normed = (
        jnp.einsum("sri,di->srd", grad_queries, query_w, preferred_element_type=jnp.float32)
        + jnp.einsum("sri,di->srd", grad_keys, key_w, preferred_element_type=jnp.float32)
        + jnp.einsum("sri,di->srd", grad_values, value_w, preferred_element_type=jnp.float32)
    )
    grad_in, g_gain_attn = norm_back(
        layer_in.astype(jnp.float32), gain_attn, grad_normed, grad_resid
    )
    factors = (
        hidden,
        grad_out,
        normed_mlp,
        grad_gate,
        grad_up,
        attn_mixed,
        grad_attn,
        normed,
        grad_queries,
        grad_keys,
        grad_values,
    )
    return (grad_in, factors, (g_gain_attn, g_gain_mlp))


def local(
    inputs, cotangent, attn_gain, w_query, w_key, w_value, w_out, mlp_gain, w_gate, w_up, w_down
):
    section_count = lax.axis_size("section")
    section_pos = lax.axis_index("section")
    block_pos = lax.axis_index("ctx")
    micro_count, seq_count, seq_rows, model_width = inputs.shape
    step_count = micro_count + section_count - 1
    places = block_pos * seq_rows + jnp.arange(seq_rows)
    cosine, sine_table = rope_tables(places)
    fetched = (
        lax.all_gather(attn_gain, "shard", axis=1, tiled=True),
        lax.all_gather(w_query, "shard", axis=1, tiled=True),
        lax.all_gather(w_key, "shard", axis=1, tiled=True),
        lax.all_gather(w_value, "shard", axis=1, tiled=True),
        lax.all_gather(w_out, "shard", axis=1, tiled=True),
        lax.all_gather(mlp_gain, "shard", axis=1, tiled=True),
        lax.all_gather(w_gate, "shard", axis=1, tiled=True),
        lax.all_gather(w_up, "shard", axis=1, tiled=True),
        lax.all_gather(w_down, "shard", axis=1, tiled=True),
    )
    weights = tuple((shard_piece[0] for shard_piece in fetched))
    received = jnp.zeros((seq_count, seq_rows, model_width), jnp.bfloat16)
    outputs = []
    stored_list = []
    for moment in range(step_count):
        layer_in = jnp.where(section_pos == 0, inputs[min(moment, micro_count - 1)], received)
        layer_out, stored = forward_layer(layer_in, weights, block_pos, cosine, sine_table)
        outputs.append(layer_out)
        stored_list.append(stored)
        if moment + 1 < step_count:
            received = shifted(layer_out, "section", 1)
    activations = lax.dynamic_slice_in_dim(jnp.stack(outputs), section_pos, micro_count, 0)
    stored_all = jax.tree.map(lambda *arrays: jnp.stack(arrays), *stored_list)
    refetched = (
        lax.all_gather(attn_gain, "shard", axis=1, tiled=True),
        lax.all_gather(w_query, "shard", axis=1, tiled=True),
        lax.all_gather(w_key, "shard", axis=1, tiled=True),
        lax.all_gather(w_value, "shard", axis=1, tiled=True),
        lax.all_gather(w_out, "shard", axis=1, tiled=True),
        lax.all_gather(mlp_gain, "shard", axis=1, tiled=True),
        lax.all_gather(w_gate, "shard", axis=1, tiled=True),
        lax.all_gather(w_up, "shard", axis=1, tiled=True),
        lax.all_gather(w_down, "shard", axis=1, tiled=True),
    )
    back_weights = tuple((shard_piece[0] for shard_piece in refetched))
    gain_totals = (jnp.zeros((model_width,), jnp.float32), jnp.zeros((model_width,), jnp.float32))
    factor_list = []
    received_grad = jnp.zeros((seq_count, seq_rows, model_width), jnp.bfloat16)
    sent_grads = []
    for moment in range(step_count):
        micro_pos = moment - (section_count - 1 - section_pos)
        is_valid = (micro_pos >= 0) & (micro_pos < micro_count)
        fwd_moment = jnp.clip(micro_pos + section_pos, 0, step_count - 1)
        stored = jax.tree.map(
            lambda member: lax.dynamic_index_in_dim(member, fwd_moment, 0, keepdims=False),
            stored_all,
        )
        grad_out = jnp.where(
            section_pos == section_count - 1, cotangent[min(moment, micro_count - 1)], received_grad
        )
        grad_out = jnp.where(is_valid, grad_out, jnp.zeros_like(grad_out))
        grad_in, factors, gain_grads = backward_layer(
            grad_out, stored, back_weights, block_pos, cosine, sine_table
        )
        gain_totals = (gain_totals[0] + gain_grads[0], gain_totals[1] + gain_grads[1])
        factor_list.append(factors)
        grad_send = grad_in.astype(jnp.bfloat16)
        sent_grads.append(grad_send)
        if moment + 1 < step_count:
            received_grad = shifted(grad_send, "section", -1)
    input_grads = lax.dynamic_slice_in_dim(
        jnp.stack(sent_grads), section_count - 1 - section_pos, micro_count, 0
    )
    joined = jax.tree.map(lambda *arrays: jnp.concatenate(arrays, 1), *factor_list)
    summed = weight_grads(joined, gain_totals)
    finals = (
        lax.psum(
            lax.psum_scatter(
                summed[0].astype(jnp.bfloat16), "shard", scatter_dimension=0, tiled=True
            ),
            "ctx",
        ).astype(jnp.float32),
        lax.psum(
            lax.psum_scatter(
                summed[1].astype(jnp.bfloat16), "shard", scatter_dimension=0, tiled=True
            ),
            "ctx",
        ).astype(jnp.float32),
        lax.psum(
            lax.psum_scatter(
                summed[2].astype(jnp.bfloat16), "shard", scatter_dimension=0, tiled=True
            ),
            "ctx",
        ).astype(jnp.float32),
        lax.psum(
            lax.psum_scatter(
                summed[3].astype(jnp.bfloat16), "shard", scatter_dimension=0, tiled=True
            ),
            "ctx",
        ).astype(jnp.float32),
        lax.psum(
            lax.psum_scatter(
                summed[4].astype(jnp.bfloat16), "shard", scatter_dimension=0, tiled=True
            ),
            "ctx",
        ).astype(jnp.float32),
        lax.psum(
            lax.psum_scatter(
                summed[5].astype(jnp.bfloat16), "shard", scatter_dimension=0, tiled=True
            ),
            "ctx",
        ).astype(jnp.float32),
        lax.psum(
            lax.psum_scatter(
                summed[6].astype(jnp.bfloat16), "shard", scatter_dimension=0, tiled=True
            ),
            "ctx",
        ).astype(jnp.float32),
        lax.psum(
            lax.psum_scatter(
                summed[7].astype(jnp.bfloat16), "shard", scatter_dimension=0, tiled=True
            ),
            "ctx",
        ).astype(jnp.float32),
        lax.psum(
            lax.psum_scatter(
                summed[8].astype(jnp.bfloat16), "shard", scatter_dimension=0, tiled=True
            ),
            "ctx",
        ).astype(jnp.float32),
    )
    return (
        activations[None],
        input_grads[None],
        finals[0][None],
        finals[1][None],
        finals[2][None],
        finals[3][None],
        finals[4][None],
        finals[5][None],
        finals[6][None],
        finals[7][None],
        finals[8][None],
    )


def solution(mesh):
    return jax.shard_map(
        local,
        mesh=mesh,
        in_specs=(
            P(None, "shard", "ctx", None),
            P(None, "shard", "ctx", None),
            P("section", "shard"),
            P("section", "shard", None),
            P("section", "shard", None),
            P("section", "shard", None),
            P("section", "shard", None),
            P("section", "shard"),
            P("section", "shard", None),
            P("section", "shard", None),
            P("section", "shard", None),
        ),
        out_specs=(
            P("section", None, "shard", "ctx", None),
            P("section", None, "shard", "ctx", None),
            P("section", "shard"),
            P("section", "shard", None),
            P("section", "shard", None),
            P("section", "shard", None),
            P("section", "shard", None),
            P("section", "shard"),
            P("section", "shard", None),
            P("section", "shard", None),
            P("section", "shard", None),
        ),
        check_vma=False,
    )
```

profile of v0, /device:TPU:0, one launch (start us, length us, event | category | flops | bytes accessed | tf_op | source)
XLA Modules:
  0.0 906.2 jit_solution(4042353581838092713)
XLA Ops:
  13.2 18.2 %all-reduce.7 = (bf16[576]{0:T(1024)(128)(2,1)S(1)}, bf16[576]{0:T(1024)(128)(2,1)S(1)}) all-reduce(bf16[576]{0:T(1024)(128)(2,1)S(1)} %dynamic-update-slice, bf16[576]{0:T(1024)(128)(2,1)S(1)} %dynamic-update-slice.1), channel_id=1, replica_groups=mesh['section'=2,'ctx'=2,'shard'=8] {'shard'}, use_global_device_ids=true, to_apply=%add | all-reduce | flops 1152 | bytes 4608
  32.7 14.9 %all_gather.57 = bf16[1,576,192]{2,1,0:T(8,128)(2,1)S(1)} all-gather(bf16[1,72,192]{2,1,0:T(8,128)(2,1)S(1)} %copy-done.164), channel_id=1, replica_groups=mesh['section'=2,'ctx'=2,'shard'=8] {'shard'}, dimensions={1}, use_global_device_ids=true | all-gather | bytes 248832 | tf_op jit(solution)/shard_map/all_gather | solution.py:274
  49.5 7.8 all-gather.1
  57.4 17.6 %all_gather.59 = bf16[1,576,576]{2,1,0:T(8,128)(2,1)S(1)} all-gather(bf16[1,72,576]{2,1,0:T(8,128)(2,1)S(1)} %copy-done.154), channel_id=1, replica_groups=mesh['section'=2,'ctx'=2,'shard'=8] {'shard'}, dimensions={1}, use_global_device_ids=true | all-gather | bytes 746496 | tf_op jit(solution)/shard_map/all_gather | solution.py:273
  76.4 14.9 %all_gather.55 = bf16[1,576,192]{2,1,0:T(8,128)(2,1)S(1)} all-gather(bf16[1,72,192]{2,1,0:T(8,128)(2,1)S(1)} %copy-done.165), channel_id=1, replica_groups=mesh['section'=2,'ctx'=2,'shard'=8] {'shard'}, dimensions={1}, use_global_device_ids=true | all-gather | bytes 248832 | tf_op jit(solution)/shard_map/all_gather | solution.py:275
  92.0 8.0 all-gather
  100.0 8.1 fusion.18
  108.2 10.2 %fusion.15 = f32[3,3,512]{2,1,0:T(4,128)S(1)} fusion(f32[3,1024,512,3]{2,1,3,0:T(8,128)} %get-tuple-element.107, f32[3,3,512]{2,1,0:T(4,128)S(1)} %get-tuple-element.106, pred[512,1024]{0,1:T(8,128)(4,1)S(1)} %iota_compare_fusion), kind=kLoop, calls=%fused_computation.33 | loop fusion | flops 18869760 | bytes 19435520 | tf_op jit(solution)/shard_map/reduce_sum | solution.py:96
  118.4 9.3 %fusion.170 = bf16[3,64,3,512]{3,1,2,0:T(8,128)(2,1)S(1)} fusion(bf16[1024,3,64,1]{0,2,3,1:T(8,128)(2,1)S(1)} %bitcast.1285, f32[3,3,512]{2,1,0:T(4,128)S(1)} %fusion.15, f32[3,3,512]{2,1,0:T(4,128)S(1)} %get-tuple-element.106, f32[3,1024,512,3]{2,1,3,0:T(8,128)} %get-tuple-element.107, pred[512,1024]{0,1:T(8,128)(4,1)S(1)} %iota_compare_fusion), kind=kOutput, calls=%fused_computation.245 | convolution fusion | flops 627867648 | bytes 20418560 | tf_op jit(solution)/shard_map/skgqj,sjkd->sqkgd/dot_general | solution.py:99
  127.8 15.3 %all_gather.60 = bf16[1,576,576]{2,1,0:T(8,128)(2,1)S(1)} all-gather(bf16[1,72,576]{2,1,0:T(8,128)(2,1)S(1)} %copy-done.155), channel_id=1, replica_groups=mesh['section'=2,'ctx'=2,'shard'=8] {'shard'}, dimensions={1}, use_global_device_ids=true | all-gather | bytes 746496 | tf_op jit(solution)/shard_map/all_gather | solution.py:276
  143.9 5.1 fusion.142
  148.9 6.4 multiply_convert_fusion.2
  162.3 13.0 %collective-permute-done = bf16[1,512,576]{1,2,0:T(8,128)(2,1)S(1)} collective-permute-done((bf16[1,512,576]{1,2,0:T(8,128)(2,1)S(1)}, bf16[1,512,576]{1,2,0:T(8,128)(2,1)S(1)}, u32[]{:S(2)}, u32[]{:S(2)}) %collective-permute-start) | collective-permute-done | bytes 589856 | tf_op jit(solution)/shard_map/ppermute | solution.py:18
  177.7 7.0 all-gather.3
  184.7 6.7 all-gather.2
  191.4 8.1 fusion.19
  199.5 10.2 %fusion.16 = f32[3,3,512]{2,1,0:T(4,128)S(1)} fusion(f32[3,1024,512,3]{2,1,3,0:T(8,128)} %get-tuple-element.113, f32[3,3,512]{2,1,0:T(4,128)S(1)} %get-tuple-element.112, pred[512,1024]{0,1:T(8,128)(4,1)S(1)} %iota_compare_fusion), kind=kLoop, calls=%fused_computation.34 | loop fusion | flops 18869760 | bytes 19435520 | tf_op jit(solution)/shard_map/reduce_sum | solution.py:96
  209.7 9.6 %fusion.173 = bf16[3,64,3,512]{3,1,2,0:T(8,128)(2,1)S(1)} fusion(bf16[1024,3,64,1]{0,2,3,1:T(8,128)(2,1)} %bitcast.1287, f32[3,3,512]{2,1,0:T(4,128)S(1)} %fusion.16, f32[3,3,512]{2,1,0:T(4,128)S(1)} %get-tuple-element.112, f32[3,1024,512,3]{2,1,3,0:T(8,128)} %get-tuple-element.113, pred[512,1024]{0,1:T(8,128)(4,1)S(1)} %iota_compare_fusion), kind=kOutput, calls=%fused_computation.246 | convolution fusion | flops 627867648 | bytes 20418560 | tf_op jit(solution)/shard_map/skgqj,sjkd->sqkgd/dot_general | solution.py:99
  228.3 5.2 collective-permute-start.1
  236.8 6.4 collective-permute-done.1
  247.2 6.3 all-gather.5
  253.6 8.3 fusion.20
  261.9 10.2 %fusion.17 = f32[3,3,512]{2,1,0:T(4,128)S(1)} fusion(f32[3,1024,512,3]{2,1,3,0:T(8,128)} %get-tuple-element.119, f32[3,3,512]{2,1,0:T(4,128)S(1)} %get-tuple-element.118, pred[512,1024]{0,1:T(8,128)(4,1)S(1)} %iota_compare_fusion), kind=kLoop, calls=%fused_computation.35 | loop fusion | flops 18869760 | bytes 19435520 | tf_op jit(solution)/shard_map/reduce_sum | solution.py:96
  272.2 6.6 all-gather.4
  278.7 9.5 %fusion.176 = bf16[3,64,3,512]{3,1,2,0:T(8,128)(2,1)S(1)} fusion(bf16[1024,3,64,1]{0,2,3,1:T(8,128)(2,1)S(1)} %bitcast.1289, f32[3,3,512]{2,1,0:T(4,128)S(1)} %fusion.17, f32[3,3,512]{2,1,0:T(4,128)S(1)} %get-tuple-element.118, f32[3,1024,512,3]{2,1,3,0:T(8,128)} %get-tuple-element.119, pred[512,1024]{0,1:T(8,128)(4,1)S(1)} %iota_compare_fusion), kind=kOutput, calls=%fused_computation.247 | convolution fusion | flops 627867648 | bytes 20418560 | tf_op jit(solution)/shard_map/skgqj,sjkd->sqkgd/dot_general | solution.py:99
  296.9 6.3 pad_maximum_fusion.1
  303.2 6.4 multiply_convert_fusion
  309.6 4.6 pad_maximum_fusion
  314.2 8.5 fusion.84
  333.1 7.9 fusion.329
  340.9 9.6 %fusion.206 = bf16[3,64,1024]{2,1,0:T(8,128)(2,1)} fusion(bf16[512,3,3,64]{0,3,2,1:T(8,128)(2,1)S(1)} %bitcast.1274, f32[3,1024,512,3]{2,1,3,0:T(8,128)} %fusion.329, f32[3,3,512]{2,1,0:T(4,128)S(1)} %get-tuple-element.94, pred[512,1024]{0,1:T(8,128)(4,1)S(1)} %iota_compare_fusion), kind=kOutput, calls=%fused_computation.267 | convolution fusion | flops 623050752 | bytes 20400128 | tf_op jit(solution)/shard_map/skgqj,sqkgd->sjkd/dot_general | solution.py:212
  350.7 13.4 %fusion.12 = (f32[3,3,512]{2,1,0:T(4,128)S(1)}, f32[3,1024,512,3]{2,1,3,0:T(8,128)}) fusion(f32[3,1024,512,3]{2,1,3,0:T(8,128)} %fusion.329, f32[3,3,512]{2,1,0:T(4,128)S(1)} %get-tuple-element.94, pred[512,1024]{0,1:T(8,128)(4,1)S(1)} %iota_compare_fusion, bf16[512,3,3,64]{0,3,2,1:T(8,128)(2,1)S(1)} %bitcast.1275, ...), kind=kOutput, calls=%fused_computation.24 | convolution fusion | flops 627568128 | bytes 39299076 | tf_op jit(solution)/shard_map/sqkgd,sjkd->skgqj/dot_general | solution.py:194
  364.1 13.5 %fusion.27 = bf16[3,3,512,1024]{2,3,1,0:T(8,128)(2,1)S(1)} fusion(f32[3,1024,512,3]{2,1,3,0:T(8,128)} %get-tuple-element.126, f32[3,1024,512,3]{2,1,3,0:T(8,128)} %fusion.329, f32[3,3,512]{2,1,0:T(4,128)S(1)} %get-tuple-element.125, f32[3,3,512]{2,1,0:T(4,128)S(1)} %get-tuple-element.94, pred[512,1024]{0,1:T(8,128)(4,1)S(1)} %iota_compare_fusion), kind=kLoop, calls=%fused_computation.45 | loop fusion | flops 28311552 | bytes 47747072 | tf_op jit(solution)/shard_map/reshape.170
  393.2 5.9 reduce-scatter.18.cloned.1.call-done
  403.3 11.7 %reduce-scatter.20.cloned.1.call-done = bf16[1,512,192]{1,2,0:T(8,128)(2,1)} async-done(((bf16[1,1024,192]{1,2,0:T(8,128)(2,1)}), bf16[1,512,192]{1,2,0:T(8,128)(2,1)}) %reduce-scatter.20.cloned.1.call-update) | async-done | bytes 196624 | tf_op jit(solution)/shard_map/reduce_scatter | solution.py:225
  419.6 9.1 %fusion.323 = f32[3,1024,512,3]{2,1,3,0:T(8,128)} fusion(bf16[3,1,512,3,3,64]{2,5,4,3,1,0:T(8,128)(2,1)S(1)} %copy-done.24, s32[]{:T(128)S(6)} %min.11, bf16[3,1,1024,3,64]{2,4,3,1,0:T(8,128)(2,1)} %copy-done.46), kind=kOutput, calls=%fused_computation.435 | convolution fusion | flops 603979776 | bytes 19858432 | tf_op jit(solution)/shard_map/sqkgd,sjkd->skgqj/dot_general | solution.py:55
  428.7 6.4 collective-permute-done.2
  435.2 5.4 fusion.75
  448.4 9.6 %fusion.209 = bf16[3,64,1024]{2,1,0:T(8,128)(2,1)} fusion(bf16[512,3,3,64]{0,3,2,1:T(8,128)(2,1)S(1)} %bitcast.1300, f32[3,1024,512,3]{2,1,3,0:T(8,128)} %fusion.323, f32[3,3,512]{2,1,0:T(4,128)S(1)} %get-tuple-element.93, pred[512,1024]{0,1:T(8,128)(4,1)S(1)} %iota_compare_fusion), kind=kOutput, calls=%fused_computation.268 | convolution fusion | flops 623050752 | bytes 20400128 | tf_op jit(solution)/shard_map/skgqj,sqkgd->sjkd/dot_general | solution.py:212
  458.0 13.0 %fusion.9 = (f32[3,3,512]{2,1,0:T(4,128)S(1)}, f32[3,1024,512,3]{2,1,3,0:T(8,128)}) fusion(f32[3,1024,512,3]{2,1,3,0:T(8,128)} %fusion.323, f32[3,3,512]{2,1,0:T(4,128)S(1)} %get-tuple-element.93, pred[512,1024]{0,1:T(8,128)(4,1)S(1)} %iota_compare_fusion, bf16[512,3,3,64]{0,3,2,1:T(8,128)(2,1)S(1)} %bitcast.1301, ...), kind=kOutput, calls=%fused_computation.19 | convolution fusion | flops 627568128 | bytes 39292932 | tf_op jit(solution)/shard_map/sqkgd,sjkd->skgqj/dot_general | solution.py:194
  471.1 13.9 %fusion.28 = bf16[3,3,512,1024]{2,3,1,0:T(8,128)(2,1)S(1)} fusion(f32[3,1024,512,3]{2,1,3,0:T(8,128)} %get-tuple-element.132, f32[3,1024,512,3]{2,1,3,0:T(8,128)} %fusion.323, f32[3,3,512]{2,1,0:T(4,128)S(1)} %get-tuple-element.131, f32[3,3,512]{2,1,0:T(4,128)S(1)} %get-tuple-element.93, pred[512,1024]{0,1:T(8,128)(4,1)S(1)} %iota_compare_fusion), kind=kLoop, calls=%fused_computation.46 | loop fusion | flops 28311552 | bytes 47747072 | tf_op jit(solution)/shard_map/reshape.209
  485.0 3.8 fusion.201
  488.9 6.7 broadcast_multiply_fusion.1
  506.5 10.7 %reduce-scatter.24.cloned.1.call-done = bf16[1,512,192]{1,2,0:T(8,128)(2,1)} async-done(((bf16[1,1024,192]{1,2,0:T(8,128)(2,1)}), bf16[1,512,192]{1,2,0:T(8,128)(2,1)}) %reduce-scatter.24.cloned.1.call-update) | async-done | bytes 196624 | tf_op jit(solution)/shard_map/reduce_scatter | solution.py:225
  523.5 7.9 fusion.318
  531.4 7.7 collective-permute-done.3
  539.2 5.5 fusion.66
  552.6 13.1 %fusion.6 = (f32[3,3,512]{2,1,0:T(4,128)S(1)}, f32[3,1024,512,3]{2,1,3,0:T(8,128)}) fusion(f32[3,1024,512,3]{2,1,3,0:T(8,128)} %fusion.318, f32[3,3,512]{2,1,0:T(4,128)S(1)} %copy-done.146, pred[512,1024]{0,1:T(8,128)(4,1)S(1)} %iota_compare_fusion, bf16[512,3,3,64]{0,3,2,1:T(8,128)(2,1)S(1)} %bitcast.1298, bf16[3,1,1024,3,64]{2,4,3,1,0:T(8,128)(2,1)} %copy-done.82, ...), kind=kOutput, calls=%fused_computation.14 | convolution fusion | flops 627568128 | bytes 39292932 | tf_op jit(solution)/shard_map/sqkgd,sjkd->skgqj/dot_general | solution.py:194
  565.8 13.7 %fusion.29 = bf16[3,3,512,1024]{2,3,1,0:T(8,128)(2,1)S(1)} fusion(f32[3,1024,512,3]{2,1,3,0:T(8,128)} %get-tuple-element.138, f32[3,1024,512,3]{2,1,3,0:T(8,128)} %fusion.318, f32[3,3,512]{2,1,0:T(4,128)S(1)} %get-tuple-element.137, f32[3,3,512]{2,1,0:T(4,128)S(1)} %copy-done.146, pred[512,1024]{0,1:T(8,128)(4,1)S(1)} %iota_compare_fusion), kind=kLoop, calls=%fused_computation.47 | loop fusion | flops 28311552 | bytes 47747072 | tf_op jit(solution)/shard_map/reshape.248
  582.2 3.7 fusion.202
  590.5 12.1 %fusion.212 = bf16[3,64,1024]{2,1,0:T(8,128)(2,1)} fusion(bf16[512,3,3,64]{0,3,2,1:T(8,128)(2,1)} %bitcast.1299, f32[3,1024,512,3]{2,1,3,0:T(8,128)} %fusion.318, f32[3,3,512]{2,1,0:T(4,128)S(1)} %copy-done.146, pred[512,1024]{0,1:T(8,128)(4,1)S(1)} %iota_compare_fusion), kind=kOutput, calls=%fused_computation.269 | convolution fusion | flops 623050752 | bytes 20400128 | tf_op jit(solution)/shard_map/skgqj,sqkgd->sjkd/dot_general | solution.py:212
  614.7 4.2 reduce-scatter.28.cloned.1.call-done
  632.5 5.3 fusion.60
  642.4 4.1 fusion.88
  646.6 6.5 fusion.89
  664.4 20.6 %reduce-scatter.40.cloned.1.call-done = bf16[72,576]{1,0:T(8,128)(2,1)} async-done(((bf16[576,576]{1,0:T(8,128)(2,1)}), bf16[72,576]{1,0:T(8,128)(2,1)}) %reduce-scatter.40.cloned.1.call-update) | async-done | bytes 82960
  685.1 35.9 %reduce-scatter.38.cloned.1.call-done = bf16[192,576]{1,0:T(8,128)(2,1)} async-done(((bf16[1536,576]{1,0:T(8,128)(2,1)}), bf16[192,576]{1,0:T(8,128)(2,1)}) %reduce-scatter.38.cloned.1.call-update) | async-done | bytes 221200 | tf_op jit(solution)/shard_map/reduce_scatter | solution.py:387
  721.0 35.6 %reduce-scatter.36.cloned.1.call-done = bf16[72,1536]{1,0:T(8,128)(2,1)} async-done(((bf16[576,1536]{1,0:T(8,128)(2,1)}), bf16[72,1536]{1,0:T(8,128)(2,1)}) %reduce-scatter.36.cloned.1.call-update) | async-done | bytes 221200 | tf_op jit(solution)/shard_map/reduce_scatter | solution.py:381
  756.6 35.4 %reduce-scatter.34.cloned.1.call-done = bf16[72,1536]{1,0:T(8,128)(2,1)} async-done(((bf16[576,1536]{1,0:T(8,128)(2,1)}), bf16[72,1536]{1,0:T(8,128)(2,1)}) %reduce-scatter.34.cloned.1.call-update) | async-done | bytes 221200 | tf_op jit(solution)/shard_map/reduce_scatter | solution.py:375
  795.2 14.2 %all-reduce.6 = (bf16[576]{0:T(1024)(128)(2,1)S(1)}, bf16[576]{0:T(1024)(128)(2,1)S(1)}) all-reduce(bf16[576]{0:T(1024)(128)(2,1)S(1)} %add_convert_fusion.4, bf16[576]{0:T(1024)(128)(2,1)S(1)} %add_convert_fusion.3), channel_id=14, replica_groups=mesh['section'=2,'ctx'=2,'shard'=8] {'shard'}, use_global_device_ids=true, to_apply=%region_36.37.clone | all-reduce | flops 1152 | bytes 4608
  811.2 12.3 %reduce-scatter.32.cloned.1.call-done = bf16[72,192]{1,0:T(8,128)(2,1)} async-done(((bf16[576,192]{1,0:T(8,128)(2,1)}), bf16[72,192]{1,0:T(8,128)(2,1)}) %reduce-scatter.32.cloned.1.call-update) | async-done | bytes 27664 | tf_op jit(solution)/shard_map/reduce_scatter | solution.py:357
  823.5 31.4 %reduce-scatter.30.cloned.1.call-done = bf16[72,192]{1,0:T(8,128)(2,1)} async-done(((bf16[576,192]{1,0:T(8,128)(2,1)}), bf16[72,192]{1,0:T(8,128)(2,1)}) %reduce-scatter.30.cloned.1.call-update) | async-done | bytes 27664 | tf_op jit(solution)/shard_map/reduce_scatter | solution.py:351
  855.0 10.1 %all-reduce.8 = (bf16[1,72]{1,0:T(2,128)(2,1)S(1)}, bf16[1,72,192]{2,1,0:T(8,128)(2,1)S(1)}, bf16[1,72,192]{2,1,0:T(8,128)(2,1)S(1)}, bf16[1,72]{1,0:T(2,128)(2,1)S(1)}) all-reduce(bf16[1,72]{1,0:T(2,128)(2,1)S(1)} %dynamic-slice_bitcast_fusion.16, ...), channel_id=1, replica_groups=mesh['section'=2,'ctx'=2,'shard'=8] {'ctx'}, use_global_device_ids=true, to_apply=%region_37.38 | all-reduce | flops 27792 | bytes 111168 | tf_op jit(solution)/shard_map/psum | solution.py:338
  867.4 25.3 %all-reduce.12.cloned.1.call-done = (bf16[1,72,576]{2,1,0:T(8,128)(2,1)}, bf16[1,72,576]{2,1,0:T(8,128)(2,1)}, bf16[1,72,1536]{2,1,0:T(8,128)(2,1)}, bf16[1,72,1536]{2,1,0:T(8,128)(2,1)}, bf16[1,192,576]{2,1,0:T(8,128)(2,1)}) async-done(((bf16[1,72,576]{2,1,0:T(8,128)(2,1)}, bf16[1,72,576]{2,1,0:T(8,128)(2,1)}, bf16[1,72,1536]{2,1,0:T(8,128)(2,1)}, bf16[1,72,1536]{2,1,0:T(8,128)(2,1)}, ...) | async-done | bytes 829456 | tf_op jit(solution)/shard_map/psum | solution.py:344
  (590 shorter events, 174.1 us)
Async XLA Ops:
  7.2 25.6 %copy-start.164 = (bf16[1,72,192]{2,1,0:T(8,128)(2,1)S(1)}, bf16[1,72,192]{2,1,0:T(8,128)(2,1)}, u32[]{:S(2)}) copy-start(bf16[1,72,192]{2,1,0:T(8,128)(2,1)} %param.15) | copy-start | bytes 82948
  7.2 136.7 %all-gather.10.cloned.1.call-start = ((), (), s32[]{:S(2)}) async-start(), calls=%async_computation.13 | async-start | bytes 1990656 | tf_op jit(solution)/shard_map/all_gather | solution.py:278
  7.9 141.0 %all-gather.12.cloned.1.call-start = ((), (), s32[]{:S(2)}) async-start(), calls=%async_computation.14 | async-start | bytes 1990656 | tf_op jit(solution)/shard_map/all_gather | solution.py:279
  8.7 146.6 %all-gather.14.cloned.1.call-start = ((), (), s32[]{:S(2)}) async-start(), calls=%async_computation.15 | async-start | bytes 2211840 | tf_op jit(solution)/shard_map/all_gather | solution.py:280
  9.4 389.7 %reduce-scatter.18.cloned.1.call-start = ((), (), s32[]{:S(2)}) async-start(), calls=%async_computation.16 | async-start | bytes 589824 | tf_op jit(solution)/shard_map/reduce_scatter | solution.py:219
  32.7 15.5 %copy-start.51 = (bf16[1,1,512,576]{2,3,1,0:T(8,128)(2,1)}, bf16[1,1,512,576]{2,3,1,0:T(8,128)(2,1)S(1)}, u32[]{:S(2)}) copy-start(bf16[1,1,512,576]{2,3,1,0:T(8,128)(2,1)S(1)} %get-tuple-element.49) | copy-start | bytes 1769476
  47.8 43.5 %copy-start.26 = (bf16[1,1,512,576]{2,3,1,0:T(8,128)(2,1)}, bf16[1,1,512,576]{2,3,1,0:T(8,128)(2,1)S(1)}, u32[]{:S(2)}) copy-start(bf16[1,1,512,576]{2,3,1,0:T(8,128)(2,1)S(1)} %fusion.258) | copy-start | bytes 1769476
  57.3 42.7 %copy-start.94 = (bf16[1024,192]{0,1:T(8,128)(2,1)}, bf16[1024,192]{0,1:T(8,128)(2,1)S(1)}, u32[]{:S(2)}) copy-start(bf16[1024,192]{0,1:T(8,128)(2,1)S(1)} %all-gather.1) | copy-start | bytes 1179652
  75.6 24.4 %copy-start.4 = (f32[512,576]{0,1:T(8,128)}, f32[512,576]{0,1:T(8,128)S(1)}, u32[]{:S(2)}) copy-start(f32[512,576]{0,1:T(8,128)S(1)} %fusion.299) | copy-start | bytes 3538948
  75.7 32.4 %copy-start.64 = (f32[1,512,9,32]{1,3,2,0:T(8,128)}, f32[1,512,9,32]{1,3,2,0:T(8,128)S(1)}, u32[]{:S(2)}) copy-start(f32[1,512,9,32]{1,3,2,0:T(8,128)S(1)} %get-tuple-element.78) | copy-start | bytes 1769476
  75.8 32.4 %copy-start.66 = (f32[1,512,9,32]{1,3,2,0:T(8,128)}, f32[1,512,9,32]{1,3,2,0:T(8,128)S(1)}, u32[]{:S(2)}) copy-start(f32[1,512,9,32]{1,3,2,0:T(8,128)S(1)} %get-tuple-element.79) | copy-start | bytes 1769476
  100.0 18.4 %copy-start.117 = (bf16[1024,192]{0,1:T(8,128)(2,1)}, bf16[1024,192]{0,1:T(8,128)(2,1)S(1)}, u32[]{:S(2)}) copy-start(bf16[1024,192]{0,1:T(8,128)(2,1)S(1)} %all-gather) | copy-start | bytes 1179652
  118.4 24.7 %copy-start.52 = (bf16[1,1,512,576]{2,3,1,0:T(8,128)(2,1)S(1)}, bf16[1,1,512,576]{2,3,1,0:T(8,128)(2,1)}, u32[]{:S(2)}) copy-start(bf16[1,1,512,576]{2,3,1,0:T(8,128)(2,1)} %copy-done.51) | copy-start | bytes 1769476
  127.8 16.1 %copy-start.102 = (bf16[3,64,3,512]{3,1,2,0:T(8,128)(2,1)}, bf16[3,64,3,512]{3,1,2,0:T(8,128)(2,1)S(1)}, u32[]{:S(2)}) copy-start(bf16[3,64,3,512]{3,1,2,0:T(8,128)(2,1)S(1)} %fusion.170) | copy-start | bytes 1769476
  143.1 184.6 %copy-start.16 = (bf16[1,576,576]{2,1,0:T(8,128)(2,1)}, bf16[1,576,576]{2,1,0:T(8,128)(2,1)S(1)}, u32[]{:S(2)}) copy-start(bf16[1,576,576]{2,1,0:T(8,128)(2,1)S(1)} %all_gather.60) | copy-start | bytes 1990660
  143.8 11.5 %copy-start.8 = (f32[512,576]{0,1:T(8,128)}, f32[512,576]{0,1:T(8,128)S(1)}, u32[]{:S(2)}) copy-start(f32[512,576]{0,1:T(8,128)S(1)} %get-tuple-element.109) | copy-start | bytes 3538948
  155.3 20.0 %copy-start.100 = (bf16[2,1,512,576]{2,3,1,0:T(8,128)(2,1)S(1)}, bf16[2,1,512,576]{2,3,1,0:T(8,128)(2,1)}, u32[]{:S(2)}) copy-start(bf16[2,1,512,576]{2,3,1,0:T(8,128)(2,1)} %param.11) | copy-start | bytes 3538948
  158.6 17.8 %copy-start.130 = (bf16[512,576]{0,1:T(8,128)(2,1)}, bf16[512,576]{0,1:T(8,128)(2,1)S(1)}, u32[]{:S(2)}) copy-start(bf16[512,576]{0,1:T(8,128)(2,1)S(1)} %fusion.179) | copy-start | bytes 1769476
  158.6 17.8 %copy-start.59 = (bf16[1,576,192]{2,1,0:T(8,128)(2,1)S(1)}, bf16[1,576,192]{2,1,0:T(8,128)(2,1)}, u32[]{:S(2)}) copy-start(bf16[1,576,192]{2,1,0:T(8,128)(2,1)} %copy-done.58) | copy-start | bytes 663556
  158.6 16.7 %collective-permute-start = (bf16[1,512,576]{1,2,0:T(8,128)(2,1)S(1)}, bf16[1,512,576]{1,2,0:T(8,128)(2,1)S(1)}, u32[]{:S(2)}, u32[]{:S(2)}) collective-permute-start(bf16[1,512,576]{1,2,0:T(8,128)(2,1)S(1)} %bitcast.1296), channel_id=1, source_target_pairs={{0,16},{1,17},{2,18},{3,19},{4,20},{5,21},{6,22},{7,23},{8,24},{9,... | collective-permute-start | bytes 1769480 | tf_op jit(solution)/shard_map/ppermute | solution.py:18
  177.5 13.9 %copy-start.68 = (f32[1,512,9,32]{1,3,2,0:T(8,128)}, f32[1,512,9,32]{1,3,2,0:T(8,128)S(1)}, u32[]{:S(2)}) copy-start(f32[1,512,9,32]{1,3,2,0:T(8,128)S(1)} %get-tuple-element.76) | copy-start | bytes 1769476
  177.5 13.9 %copy-start.70 = (f32[1,512,9,32]{1,3,2,0:T(8,128)}, f32[1,512,9,32]{1,3,2,0:T(8,128)S(1)}, u32[]{:S(2)}) copy-start(f32[1,512,9,32]{1,3,2,0:T(8,128)S(1)} %get-tuple-element.77) | copy-start | bytes 1769476
  184.7 14.8 %copy-start.96 = (bf16[1024,192]{0,1:T(8,128)(2,1)}, bf16[1024,192]{0,1:T(8,128)(2,1)S(1)}, u32[]{:S(2)}) copy-start(bf16[1024,192]{0,1:T(8,128)(2,1)S(1)} %all-gather.3) | copy-start | bytes 1179652
  209.7 9.6 %copy-start.29 = (bf16[1,512,576]{1,2,0:T(8,128)(2,1)S(1)}, bf16[1,512,576]{1,2,0:T(8,128)(2,1)}, u32[]{:S(2)}) copy-start(bf16[1,512,576]{1,2,0:T(8,128)(2,1)} %copy-done.28) | copy-start | bytes 1769476
  228.3 14.9 %collective-permute-start.1 = (bf16[1,512,576]{1,2,0:T(8,128)(2,1)}, bf16[1,512,576]{1,2,0:T(8,128)(2,1)}, u32[]{:S(2)}, u32[]{:S(2)}) collective-permute-start(bf16[1,512,576]{1,2,0:T(8,128)(2,1)} %fusion.182), channel_id=1, source_target_pairs={{0,16},{1,17},{2,18},{3,19},{4,20},{5,21},{6,22},{7,23},{8,24},{9,... | collective-permute-start | bytes 1769480 | tf_op jit(solution)/shard_map/ppermute | solution.py:18
  247.0 14.9 %copy-start.72 = (f32[1,512,9,32]{1,3,2,0:T(8,128)}, f32[1,512,9,32]{1,3,2,0:T(8,128)S(1)}, u32[]{:S(2)}) copy-start(f32[1,512,9,32]{1,3,2,0:T(8,128)S(1)} %get-tuple-element.74) | copy-start | bytes 1769476
  247.0 14.8 %copy-start.74 = (f32[1,512,9,32]{1,3,2,0:T(8,128)}, f32[1,512,9,32]{1,3,2,0:T(8,128)S(1)}, u32[]{:S(2)}) copy-start(f32[1,512,9,32]{1,3,2,0:T(8,128)S(1)} %get-tuple-element.75) | copy-start | bytes 1769476
  289.0 14.2 %copy-start.14 = (f32[1,512,576]{1,2,0:T(8,128)}, f32[1,512,576]{1,2,0:T(8,128)S(1)}, u32[]{:S(2)}) copy-start(f32[1,512,576]{1,2,0:T(8,128)S(1)} %get-tuple-element.121) | copy-start | bytes 3538948
  289.0 14.2 %copy-start.162 = (f32[512]{0:T(512)}, f32[512]{0:T(512)S(1)}, u32[]{:S(2)}) copy-start(f32[512]{0:T(512)S(1)} %add_rsqrt_fusion.6) | copy-start | bytes 6148
  290.9 35.5 %copy-start.1 = (f32[3,1,512,576]{2,3,1,0:T(8,128)}, f32[3,1,512,576]{2,3,1,0:T(8,128)S(1)}, u32[]{:S(2)}) copy-start(f32[3,1,512,576]{2,3,1,0:T(8,128)S(1)} %pad_maximum_fusion.3) | copy-start | bytes 10616836
  331.2 46.4 %copy-start.23 = (bf16[3,1,512,3,3,64]{2,5,4,3,1,0:T(8,128)(2,1)}, bf16[3,1,512,3,3,64]{2,5,4,3,1,0:T(8,128)(2,1)S(1)}, u32[]{:S(2)}) copy-start(bf16[3,1,512,3,3,64]{2,5,4,3,1,0:T(8,128)(2,1)S(1)} %pad_maximum_fusion.5) | copy-start | bytes 5308420
  333.0 48.3 %copy-start.46 = (bf16[3,1,1024,3,64]{2,4,3,1,0:T(8,128)(2,1)}, bf16[3,1,1024,3,64]{2,4,3,1,0:T(8,128)(2,1)S(1)}, u32[]{:S(2)}) copy-start(bf16[3,1,1024,3,64]{2,4,3,1,0:T(8,128)(2,1)S(1)} %pad_maximum_fusion.9) | copy-start | bytes 3538948
  340.9 9.7 %copy-start.118 = (bf16[1024,192]{0,1:T(8,128)(2,1)S(1)}, bf16[1024,192]{0,1:T(8,128)(2,1)}, u32[]{:S(2)}) copy-start(bf16[1024,192]{0,1:T(8,128)(2,1)} %copy-done.117) | copy-start | bytes 1179652
  340.9 9.7 %copy-start.119 = (bf16[1024,192]{0,1:T(8,128)(2,1)S(1)}, bf16[1024,192]{0,1:T(8,128)(2,1)}, u32[]{:S(2)}) copy-start(bf16[1024,192]{0,1:T(8,128)(2,1)} %all-gather.2) | copy-start | bytes 1179652
  350.7 13.4 %copy-start.82 = (bf16[3,1,1024,3,64]{2,4,3,1,0:T(8,128)(2,1)}, bf16[3,1,1024,3,64]{2,4,3,1,0:T(8,128)(2,1)S(1)}, u32[]{:S(2)}) copy-start(bf16[3,1,1024,3,64]{2,4,3,1,0:T(8,128)(2,1)S(1)} %pad_maximum_fusion.10) | copy-start | bytes 3538948
  384.2 30.8 %reduce-scatter.20.cloned.1.call-start = ((), (), s32[]{:S(2)}) async-start(), calls=%async_computation.17 | async-start | bytes 589824 | tf_op jit(solution)/shard_map/reduce_scatter | solution.py:225
  390.2 112.1 %reduce-scatter.22.cloned.1.call-start = ((), (), s32[]{:S(2)}) async-start(), calls=%async_computation.18 | async-start | bytes 589824 | tf_op jit(solution)/shard_map/reduce_scatter | solution.py:219
  418.0 10.7 %copy-start.107 = (bf16[512,576]{0,1:T(8,128)(2,1)}, bf16[512,576]{0,1:T(8,128)(2,1)S(1)}, u32[]{:S(2)}) copy-start(bf16[512,576]{0,1:T(8,128)(2,1)S(1)} %fusion.224) | copy-start | bytes 1769476
  418.0 17.1 %copy-start.86 = (bf16[2,1,512,576]{2,3,1,0:T(8,128)(2,1)S(1)}, bf16[2,1,512,576]{2,3,1,0:T(8,128)(2,1)}, u32[]{:S(2)}) copy-start(bf16[2,1,512,576]{2,3,1,0:T(8,128)(2,1)} %param.12) | copy-start | bytes 3538948
  418.0 17.1 %collective-permute-start.2 = (bf16[1,512,576]{1,2,0:T(8,128)(2,1)S(1)}, bf16[1,512,576]{1,2,0:T(8,128)(2,1)S(1)}, u32[]{:S(2)}, u32[]{:S(2)}) collective-permute-start(bf16[1,512,576]{1,2,0:T(8,128)(2,1)S(1)} %bitcast.1272), channel_id=1, source_target_pairs={{16,0},{17,1},{18,2},{19,3},{20,4},{21,5},{22,6},{23,7},{24,8},{25... | collective-permute-start | bytes 1769480 | tf_op jit(solution)/shard_map/ppermute | solution.py:18
  419.6 15.6 %copy-start.177 = (bf16[1,1536,576]{2,1,0:T(8,128)(2,1)S(1)}, bf16[1,1536,576]{2,1,0:T(8,128)(2,1)}, u32[]{:S(2)}) copy-start(bf16[1,1536,576]{2,1,0:T(8,128)(2,1)} %all-gather.14.cloned.1.call-done) | copy-start | bytes 5308420
  435.2 11.1 %copy-start.79 = (bf16[1,512,576]{1,2,0:T(8,128)(2,1)}, bf16[1,512,576]{1,2,0:T(8,128)(2,1)S(1)}, u32[]{:S(2)}) copy-start(bf16[1,512,576]{1,2,0:T(8,128)(2,1)S(1)} %fusion.326) | copy-start | bytes 1769476
  447.8 10.2 %copy-start.141 = (bf16[1,512,576]{1,2,0:T(8,128)(2,1)}, bf16[1,512,576]{1,2,0:T(8,128)(2,1)S(1)}, u32[]{:S(2)}) copy-start(bf16[1,512,576]{1,2,0:T(8,128)(2,1)S(1)} %fusion.450) | copy-start | bytes 1769476
  488.8 28.4 %reduce-scatter.24.cloned.1.call-start = ((), (), s32[]{:S(2)}) async-start(), calls=%async_computation.19 | async-start | bytes 589824 | tf_op jit(solution)/shard_map/reduce_scatter | solution.py:225
  497.8 111.4 %reduce-scatter.26.cloned.1.call-start = ((), (), s32[]{:S(2)}) async-start(), calls=%async_computation.20 | async-start | bytes 589824 | tf_op jit(solution)/shard_map/reduce_scatter | solution.py:219
  522.1 17.1 %copy-start.87 = (bf16[2,1,512,576]{2,3,1,0:T(8,128)(2,1)S(1)}, bf16[2,1,512,576]{2,3,1,0:T(8,128)(2,1)}, u32[]{:S(2)}) copy-start(bf16[2,1,512,576]{2,3,1,0:T(8,128)(2,1)} %param.12) | copy-start | bytes 3538948
  522.1 17.1 %collective-permute-start.3 = (bf16[1,512,576]{1,2,0:T(8,128)(2,1)S(1)}, bf16[1,512,576]{1,2,0:T(8,128)(2,1)S(1)}, u32[]{:S(2)}, u32[]{:S(2)}) collective-permute-start(bf16[1,512,576]{1,2,0:T(8,128)(2,1)S(1)} %fusion.236), channel_id=1, source_target_pairs={{16,0},{17,1},{18,2},{19,3},{20,4},{21,5},{22,6},{23,7},{24,8},{25... | collective-permute-start | bytes 1769480 | tf_op jit(solution)/shard_map/ppermute | solution.py:18
  523.5 15.7 %copy-start.178 = (bf16[1,1536,576]{2,1,0:T(8,128)(2,1)S(1)}, bf16[1,1536,576]{2,1,0:T(8,128)(2,1)}, u32[]{:S(2)}) copy-start(bf16[1,1536,576]{2,1,0:T(8,128)(2,1)} %all-gather.14.cloned.1.call-done) | copy-start | bytes 5308420
  539.2 11.2 %copy-start.76 = (bf16[1,512,576]{1,2,0:T(8,128)(2,1)}, bf16[1,512,576]{1,2,0:T(8,128)(2,1)S(1)}, u32[]{:S(2)}) copy-start(bf16[1,512,576]{1,2,0:T(8,128)(2,1)S(1)} %fusion.327) | copy-start | bytes 1769476
  551.9 13.9 %copy-start.143 = (bf16[1,512,576]{1,2,0:T(8,128)(2,1)}, bf16[1,512,576]{1,2,0:T(8,128)(2,1)S(1)}, u32[]{:S(2)}) copy-start(bf16[1,512,576]{1,2,0:T(8,128)(2,1)S(1)} %fusion.451) | copy-start | bytes 1769476
  552.5 13.3 %copy-start.145 = (bf16[512,576]{0,1:T(8,128)(2,1)}, bf16[512,576]{0,1:T(8,128)(2,1)S(1)}, u32[]{:S(2)}) copy-start(bf16[512,576]{0,1:T(8,128)(2,1)S(1)} %convolution_convert_fusion) | copy-start | bytes 1769476
  590.4 28.4 %reduce-scatter.28.cloned.1.call-start = ((), (), s32[]{:S(2)}) async-start(), calls=%async_computation.21 | async-start | bytes 589824 | tf_op jit(solution)/shard_map/reduce_scatter | solution.py:225
  602.6 61.9 %reduce-scatter.42.cloned.1.call-start = ((), (), s32[]{:S(2)}) async-start(), calls=%async_computation.28 | async-start | bytes 829440
  608.9 76.2 %reduce-scatter.40.cloned.1.call-start = ((), (), s32[]{:S(2)}) async-start(), calls=%async_computation.27 | async-start | bytes 829440
  629.3 91.7 %reduce-scatter.38.cloned.1.call-start = ((), (), s32[]{:S(2)}) async-start(), calls=%async_computation.26 | async-start | bytes 2211840 | tf_op jit(solution)/shard_map/reduce_scatter | solution.py:387
  637.8 118.8 %reduce-scatter.36.cloned.1.call-start = ((), (), s32[]{:S(2)}) async-start(), calls=%async_computation.25 | async-start | bytes 1990656 | tf_op jit(solution)/shard_map/reduce_scatter | solution.py:381
  646.5 145.5 %reduce-scatter.34.cloned.1.call-start = ((), (), s32[]{:S(2)}) async-start(), calls=%async_computation.24 | async-start | bytes 1990656 | tf_op jit(solution)/shard_map/reduce_scatter | solution.py:375
  653.1 170.4 %reduce-scatter.32.cloned.1.call-start = ((), (), s32[]{:S(2)}) async-start(), calls=%async_computation.23 | async-start | bytes 331776 | tf_op jit(solution)/shard_map/reduce_scatter | solution.py:357
  656.9 198.1 %reduce-scatter.30.cloned.1.call-start = ((), (), s32[]{:S(2)}) async-start(), calls=%async_computation.22 | async-start | bytes 331776 | tf_op jit(solution)/shard_map/reduce_scatter | solution.py:351
  660.2 232.6 %all-reduce.12.cloned.1.call-start = ((), (), s32[]{:S(2)}) async-start(), calls=%async_computation.29 | async-start | bytes 1744896 | tf_op jit(solution)/shard_map/psum | solution.py:344
  660.9 131.2 %copy-start.131 = (bf16[512,576]{0,1:T(8,128)(2,1)S(1)}, bf16[512,576]{0,1:T(8,128)(2,1)}, u32[]{:S(2)}) copy-start(bf16[512,576]{0,1:T(8,128)(2,1)} %copy-done.130) | copy-start | bytes 1769476
  792.1 17.5 %copy-start.101 = (bf16[1,1,512,576]{2,3,1,0:T(8,128)(2,1)S(1)}, bf16[1,1,512,576]{2,3,1,0:T(8,128)(2,1)}, u32[]{:S(2)}) copy-start(bf16[1,1,512,576]{2,3,1,0:T(8,128)(2,1)} %get-tuple-element.101) | copy-start | bytes 1769476
  792.1 17.5 %copy-start.106 = (bf16[1,512,576]{1,2,0:T(8,128)(2,1)S(1)}, bf16[1,512,576]{1,2,0:T(8,128)(2,1)}, u32[]{:S(2)}) copy-start(bf16[1,512,576]{1,2,0:T(8,128)(2,1)} %copy-done.105) | copy-start | bytes 1769476
  792.1 17.5 %copy-start.108 = (bf16[512,576]{0,1:T(8,128)(2,1)S(1)}, bf16[512,576]{0,1:T(8,128)(2,1)}, u32[]{:S(2)}) copy-start(bf16[512,576]{0,1:T(8,128)(2,1)} %copy-done.107) | copy-start | bytes 1769476
  (149 other events, 433.1 us)
Sparse Core Ops, SparseCore 0:
  9.7 30.5 all-gather.9
  41.9 31.4 all-gather.11
  75.1 28.0 all-gather.13
  384.3 14.7 reduce-scatter.17
  401.8 13.1 reduce-scatter.19
  489.0 12.1 reduce-scatter.21
  504.1 13.1 reduce-scatter.23
  590.5 12.2 reduce-scatter.25
  605.7 13.1 reduce-scatter.27
  621.0 31.6 reduce-scatter.41
  655.1 29.8 reduce-scatter.39
  687.3 33.7 reduce-scatter.37
  723.4 33.1 reduce-scatter.35
  758.9 33.0 reduce-scatter.33
  794.8 28.6 reduce-scatter.31
  826.2 28.7 reduce-scatter.29
  857.6 35.0 all-reduce.11
where the time goes:
time: 912 us; the launch traced here: 906 us
  matrix products  289 us (32%)
  waiting for transfers between devices  265 us (29%)
  blocking collectives  148 us (16%)
  other arithmetic  133 us (15%)
  local copies, waits for them, and re-layouts  40.4 us (4%)
  between operations  18 us (2%)
  starting transfers between devices  13.1 us (1%)
    dot_general x6, matrix products, attention_scores(): jnp.einsum('sqkgd,sjkd->skgqj', queries, keys_all, preferred_element_type...  49.3 us
    another operation x3, other arithmetic  41 us
    dot_general x3, matrix products, backward_layer(): jnp.einsum('sqkgd,sjkd->skgqj', grad_mixed, values_all, preferred_element...  39.6 us
    reduce_scatter x1, waiting for transfers between devices, local(): lax.psum_scatter(summed[8].astype(jnp.bfloat16), 'shard', scatter_dimensi...  35.9 us
    reduce_scatter x1, waiting for transfers between devices, local(): lax.psum_scatter(summed[7].astype(jnp.bfloat16), 'shard', scatter_dimensi...  35.6 us
    reduce_scatter x1, waiting for transfers between devices, local(): lax.psum_scatter(summed[6].astype(jnp.bfloat16), 'shard', scatter_dimensi...  35.4 us
    unnamed x389, local copies, waits for them, and re-layouts  34.9 us
    ppermute x4, waiting for transfers between devices, shifted(): return lax.ppermute(x, axis, pairs)  33.5 us
  transfers between devices with their start and end apart: 21, of which 15 were waited for; matrix products, arithmetic and copies ran while one was open for 18% of the time, Pallas kernels for 0%

commit v1 on v0

v1 whole, which is shorter than its diff:
```python
import functools

import jax
import jax.numpy as jnp
from jax import lax
from jax.experimental import pallas as pl
from jax.experimental.pallas import tpu as pltpu
from jax.sharding import PartitionSpec as P

HEADS = 9
KV_HEADS = 3
HEAD_DIM = 64
GROUPS = HEADS // KV_HEADS

epsilon = 1e-05
rope_base = 100000.0
f32 = jnp.float32
bf16 = jnp.bfloat16


def rope_tables(positions):
    half_dim = HEAD_DIM // 2
    frequency = rope_base ** (-(jnp.arange(half_dim).astype(f32) * 2.0 / HEAD_DIM))
    angles = frequency[:, None] * positions.astype(f32)[None, :]
    return jnp.cos(angles), jnp.sin(angles)


def rotate(source, cosine, sine):
    rows = source.shape[-1]
    pairs = source.reshape(-1, 2, HEAD_DIM // 2, rows)
    first, second = pairs[:, 0], pairs[:, 1]
    turned = jnp.stack(
        [first * cosine - second * sine, second * cosine + first * sine], axis=1
    )
    return turned.reshape(source.shape)


def inverse_rms(source):
    return lax.rsqrt(jnp.mean(source * source, -1, keepdims=True) + epsilon)


def norm_back(source, gain_vec, grad_normed, grad_carry):
    factor = inverse_rms(source)
    unit_rows = source * factor
    gain_grad = jnp.sum(grad_normed * unit_rows, axis=0)
    scaled = grad_normed * gain_vec
    back = factor * (scaled - unit_rows * jnp.mean(scaled * unit_rows, -1, keepdims=True))
    return grad_carry + back, gain_grad


def dot(left, right, left_dim, right_dim):
    return lax.dot_general(
        left, right, (((left_dim,), (right_dim,)), ((), ())), preferred_element_type=f32
    )


def visible(keys, rows):
    return lax.broadcasted_iota(jnp.int32, (keys, rows), 0) <= lax.broadcasted_iota(
        jnp.int32, (keys, rows), 1
    )


def attend_kernel(blocks, pos_ref, q_ref, kv_ref, mixed_ref, log_ref, acc_ref):
    rows = q_ref.shape[-1]
    here = pos_ref[0]
    width = KV_HEADS * HEAD_DIM
    shown = visible(rows, rows)

    def one_kv(kv):
        row0 = pl.multiple_of(kv * HEAD_DIM, HEAD_DIM)
        for g in range(GROUPS):
            q0 = pl.multiple_of((kv * GROUPS + g) * HEAD_DIM, HEAD_DIM)
            q = q_ref[pl.ds(q0, HEAD_DIM), :]

            def scores_at(c):
                k = kv_ref[c, pl.ds(row0, HEAD_DIM), :]
                return dot(k, q, 0, 0)

            s = jnp.where(shown, scores_at(here), -1e30)
            top = jnp.max(s, axis=0, keepdims=True)
            e = jnp.exp(s - top)
            total = jnp.sum(e, axis=0, keepdims=True)
            v = kv_ref[here, pl.ds(width + row0, HEAD_DIM), :]
            acc_ref[...] = dot(v, e.astype(bf16), 1, 0)

            def earlier(c, carry):
                top, total = carry
                s = scores_at(c)
                new_top = jnp.maximum(top, jnp.max(s, axis=0, keepdims=True))
                fade = jnp.exp(top - new_top)
                e = jnp.exp(s - new_top)
                v = kv_ref[c, pl.ds(width + row0, HEAD_DIM), :]
                acc_ref[...] = acc_ref[...] * fade + dot(v, e.astype(bf16), 1, 0)
                return new_top, total * fade + jnp.sum(e, axis=0, keepdims=True)

            top, total = lax.fori_loop(0, here, earlier, (top, total))
            mixed_ref[pl.ds(q0, HEAD_DIM), :] = (acc_ref[...] / total).astype(bf16)
            log_ref[pl.ds(kv * GROUPS + g, 1), :] = top + jnp.log(total)

    pl.loop(0, KV_HEADS)(one_kv)


def attend(pos, q, kv):
    blocks, _, rows = kv.shape
    vmem = pl.BlockSpec(memory_space=pltpu.VMEM)
    pairs = HEADS * rows * rows * blocks
    return pl.pallas_call(
        functools.partial(attend_kernel, blocks),
        out_shape=(
            jax.ShapeDtypeStruct(q.shape, bf16),
            jax.ShapeDtypeStruct((16, rows), f32),
        ),
        in_specs=[pl.BlockSpec(memory_space=pltpu.SMEM), vmem, vmem],
        out_specs=(vmem, vmem),
        scratch_shapes=[pltpu.VMEM((HEAD_DIM, rows), f32)],
        compiler_params=pltpu.CompilerParams(vmem_limit_bytes=40 * 2**20),
        cost_estimate=pl.CostEstimate(
            flops=16 * pairs * HEAD_DIM, bytes_accessed=4 * 2**20, transcendentals=pairs
        ),
    )(pos, q, kv)


def attend_back_kernel(blocks, pos_ref, q_ref, kv_ref, log_ref, dm_ref, dq_ref, dkv_ref,
                       keep_p, keep_d, acc_ref):
    rows = q_ref.shape[-1]
    here = pos_ref[0]
    width = KV_HEADS * HEAD_DIM
    shown = visible(rows, rows)
    dkv_ref[...] = jnp.zeros_like(dkv_ref)

    def one_kv(kv):
        row0 = pl.multiple_of(kv * HEAD_DIM, HEAD_DIM)
        for g in range(GROUPS):
            q0 = pl.multiple_of((kv * GROUPS + g) * HEAD_DIM, HEAD_DIM)
            q = q_ref[pl.ds(q0, HEAD_DIM), :]
            dm = dm_ref[pl.ds(q0, HEAD_DIM), :]
            log_total = log_ref[pl.ds(kv * GROUPS + g, 1), :]

            def first_pass(c, masked):
                k = kv_ref[c, pl.ds(row0, HEAD_DIM), :]
                v = kv_ref[c, pl.ds(width + row0, HEAD_DIM), :]
                p = jnp.exp(dot(k, q, 0, 0) - log_total)
                if masked:
                    p = jnp.where(shown, p, 0.0)
                d = dot(v, dm, 0, 0)
                keep_p[c] = p
                keep_d[c] = d
                return jnp.sum(p * d, axis=0, keepdims=True)

            delta = first_pass(here, True)
            delta = lax.fori_loop(0, here, lambda c, t: t + first_pass(c, False), delta)
            acc_ref[...] = jnp.zeros_like(acc_ref)

            def second_pass(c, _):
                p = keep_p[c]
                ds = (p * (keep_d[c] - delta)).astype(bf16)
                k = kv_ref[c, pl.ds(row0, HEAD_DIM), :]
                acc_ref[...] += dot(k, ds, 1, 0)
                dkv_ref[c, pl.ds(row0, HEAD_DIM), :] += dot(q, ds, 1, 1)
                dkv_ref[c, pl.ds(width + row0, HEAD_DIM), :] += dot(dm, p.astype(bf16), 1, 1)
                return 0

            lax.fori_loop(0, here + 1, second_pass, 0)
            dq_ref[pl.ds(q0, HEAD_DIM), :] = acc_ref[...]

    pl.loop(0, KV_HEADS)(one_kv)


def attend_back(pos, q, kv, log_total, dm):
    blocks, _, rows = kv.shape
    vmem = pl.BlockSpec(memory_space=pltpu.VMEM)
    pairs = HEADS * rows * rows * blocks
    return pl.pallas_call(
        functools.partial(attend_back_kernel, blocks),
        out_shape=(
            jax.ShapeDtypeStruct(q.shape, f32),
            jax.ShapeDtypeStruct(kv.shape, f32),
        ),
        in_specs=[pl.BlockSpec(memory_space=pltpu.SMEM)] + [vmem] * 4,
        out_specs=(vmem, vmem),
        scratch_shapes=[
            pltpu.VMEM((blocks, rows, rows), f32),
            pltpu.VMEM((blocks, rows, rows), f32),
            pltpu.VMEM((HEAD_DIM, rows), f32),
        ],
        compiler_params=pltpu.CompilerParams(vmem_limit_bytes=40 * 2**20),
        cost_estimate=pl.CostEstimate(
            flops=40 * pairs * HEAD_DIM, bytes_accessed=8 * 2**20, transcendentals=pairs
        ),
    )(pos, q, kv, log_total, dm)


def exchange(x, axis, bit=1):
    return lax.ppermute(x, axis, [(i, i ^ bit) for i in range(lax.axis_size(axis))])


def gathered(piece):
    return lax.all_gather(piece, "shard", axis=0, tiled=True)


def reduce_rows(grad):
    devices = lax.axis_size("shard")
    me = lax.axis_index("shard")
    part = grad.astype(bf16).reshape(devices, -1, grad.shape[-1])
    bit = 1
    while bit < devices:
        mine = (me // bit) % 2
        halves = part.reshape(part.shape[0] // 2, 2, *part.shape[1:])
        keep = lax.dynamic_index_in_dim(halves, mine, 1, keepdims=False)
        send = lax.dynamic_index_in_dim(halves, 1 - mine, 1, keepdims=False)
        part = (keep.astype(f32) + exchange(send, "shard", bit).astype(f32)).astype(bf16)
        bit *= 2
    return part[0]


def sum_ctx(part):
    if lax.axis_size("ctx") == 2:
        return part.astype(f32) + exchange(part, "ctx").astype(f32)
    return lax.psum(part, "ctx").astype(f32)


def forward_layer(layer_in, weights, pos, cosine, sine):
    gain_attn, gain_mlp, qkv_w, out_w, gate_up_w, down_w = weights
    hidden_in = layer_in.astype(f32)
    normed = (hidden_in * inverse_rms(hidden_in) * gain_attn).astype(bf16)
    raw = dot(qkv_w, normed, 0, 1)
    q_width = HEADS * HEAD_DIM
    kv_width = KV_HEADS * HEAD_DIM
    queries = (rotate(raw[:q_width], cosine, sine).astype(bf16) * HEAD_DIM**-0.5).astype(bf16)
    keys = rotate(raw[q_width : q_width + kv_width], cosine, sine).astype(bf16)
    values = raw[q_width + kv_width :].astype(bf16)
    kv = lax.all_gather(jnp.concatenate([keys, values], 0), "ctx", axis=0)
    mixed, log_total = attend(pos, queries, kv)
    residual = hidden_in + dot(mixed, out_w, 0, 0)
    normed_mlp = (residual * inverse_rms(residual) * gain_mlp).astype(bf16)
    gate_up = dot(normed_mlp, gate_up_w, 1, 0)
    ff = gate_up.shape[-1] // 2
    gate, up = gate_up[:, :ff], gate_up[:, ff:]
    hidden = (gate * jax.nn.sigmoid(gate) * up).astype(bf16)
    layer_out = (residual + dot(hidden, down_w, 1, 0)).astype(bf16)
    stored = (layer_in, normed, queries, kv, log_total, mixed, residual, normed_mlp, gate_up, hidden)
    return layer_out, stored


def backward_layer(grad_out, stored, weights, pos, cosine, sine):
    gain_attn, gain_mlp, qkv_w, out_w, gate_up_w, down_w = weights
    layer_in, normed, queries, kv, log_total, mixed, residual, normed_mlp, gate_up, hidden = stored
    ff = gate_up.shape[-1] // 2
    gate, up = gate_up[:, :ff], gate_up[:, ff:]
    g_down = dot(hidden, grad_out, 0, 0)
    d_hidden = dot(grad_out, down_w, 1, 1)
    sig = jax.nn.sigmoid(gate)
    d_gate = (d_hidden * up * sig * (1.0 + gate * (1.0 - sig))).astype(bf16)
    d_up = (d_hidden * gate * sig).astype(bf16)
    d_gate_up = jnp.concatenate([d_gate, d_up], 1)
    g_gate_up = dot(normed_mlp, d_gate_up, 0, 0)
    d_normed = dot(d_gate_up, gate_up_w, 1, 1)
    d_res, g_gain_mlp = norm_back(residual, gain_mlp, d_normed, grad_out.astype(f32))
    d_attn = d_res.astype(bf16)
    g_out = dot(mixed, d_attn, 1, 0)
    d_mixed = dot(out_w, d_attn, 1, 1).astype(bf16)
    d_queries, d_kv = attend_back(pos, queries, kv, log_total, d_mixed)
    d_kv = d_kv.astype(bf16)
    if lax.axis_size("ctx") == 2:
        me = lax.axis_index("ctx")
        own = lax.dynamic_index_in_dim(d_kv, me, 0, keepdims=False).astype(f32)
        other = lax.dynamic_index_in_dim(d_kv, 1 - me, 0, keepdims=False)
        d_kv = own + exchange(other, "ctx").astype(f32)
    else:
        d_kv = lax.psum_scatter(d_kv, "ctx", scatter_dimension=0).astype(f32)
    kv_width = KV_HEADS * HEAD_DIM
    d_q = rotate(d_queries * HEAD_DIM**-0.5, cosine, -sine).astype(bf16)
    d_k = rotate(d_kv[:kv_width], cosine, -sine).astype(bf16)
    d_v = d_kv[kv_width:].astype(bf16)
    d_qkv = jnp.concatenate([d_q, d_k, d_v], 0)
    g_qkv = dot(normed, d_qkv, 0, 1)
    d_n = dot(d_qkv, qkv_w, 0, 1)
    grad_in, g_gain_attn = norm_back(layer_in.astype(f32), gain_attn, d_n, d_res)
    gains = jnp.stack([g_gain_attn, g_gain_mlp], 1)
    late = jnp.concatenate([g_qkv, gains], 1)
    return grad_in.astype(bf16), (g_down, g_gate_up, g_out, late)


def local(
    inputs, cotangent, attn_gain, w_query, w_key, w_value, w_out, mlp_gain, w_gate, w_up, w_down
):
    layers = lax.axis_size("section")
    section = lax.axis_index("section")
    block_pos = lax.axis_index("ctx")
    _, _, rows, width = inputs.shape
    pos = jnp.reshape(block_pos, (1,)).astype(jnp.int32)
    cosine, sine = rope_tables(block_pos * rows + jnp.arange(rows))
    qkv_cols = w_query.shape[-1] + w_key.shape[-1] + w_value.shape[-1]

    early = jnp.concatenate(
        [w_query[0], w_key[0], w_value[0], attn_gain[0][:, None], mlp_gain[0][:, None]], 1
    )
    pieces = (early, w_out[0], jnp.concatenate([w_gate[0], w_up[0]], 1), w_down[0])

    def both(piece):
        other = exchange(piece, "section")
        return [jnp.where(section == l, piece, other) for l in range(layers)]

    shards = [both(piece) for piece in pieces]
    weights = []
    for l in range(layers):
        early_all, out_all, gate_up_all, down_all = [gathered(s[l]) for s in shards]
        gains = early_all[:, qkv_cols:].astype(f32).T
        weights.append(
            (gains[0:1], gains[1:2], early_all[:, :qkv_cols], out_all, gate_up_all, down_all)
        )

    hidden_now = lax.dynamic_index_in_dim(inputs, section, 0, keepdims=False)[0]
    outs, kept = [], []
    for l in range(layers):
        hidden_now, stored = forward_layer(hidden_now, weights[l], pos, cosine, sine)
        outs.append(hidden_now)
        kept.append(stored)

    grad = lax.dynamic_index_in_dim(cotangent, section, 0, keepdims=False)[0]
    in_grads, parts = [None] * layers, [None] * layers
    for l in reversed(range(layers)):
        grad, raw = backward_layer(grad, kept[l], weights[l], pos, cosine, sine)
        in_grads[l] = grad
        parts[l] = [reduce_rows(g) for g in raw]

    def swap(per_layer):
        mine = jnp.where(section == 0, per_layer[0], per_layer[1])
        other = exchange(jnp.where(section == 0, per_layer[1], per_layer[0]), "section")
        return mine, other

    def both_micro(per_layer):
        mine, other = swap(per_layer)
        first = jnp.where(section == 0, mine, other)
        second = jnp.where(section == 0, other, mine)
        return jnp.stack([first, second])[None, :, None]

    finals = []
    for pair in zip(*parts):
        mine, other = swap(pair)
        finals.append(sum_ctx((mine.astype(f32) + other.astype(f32)).astype(bf16)))
    g_down, g_gate_up, g_out, late = finals
    ff = w_gate.shape[-1]
    a, b = w_query.shape[-1], w_query.shape[-1] + w_key.shape[-1]
    return (
        both_micro(outs),
        both_micro(in_grads),
        late[None, :, qkv_cols],
        late[None, :, :a],
        late[None, :, a:b],
        late[None, :, b:qkv_cols],
        g_out[None],
        late[None, :, qkv_cols + 1],
        g_gate_up[None, :, :ff],
        g_gate_up[None, :, ff:],
        g_down[None],
    )


def solution(mesh):
    tokens = P(None, "shard", "ctx", None)
    gain = P("section", "shard")
    matrix = P("section", "shard", None)
    result = P("section", None, "shard", "ctx", None)
    return jax.shard_map(
        local,
        mesh=mesh,
        in_specs=(tokens, tokens, gain, matrix, matrix, matrix, matrix, gain, matrix, matrix, matrix),
        out_specs=(result, result, gain, matrix, matrix, matrix, matrix, gain, matrix, matrix, matrix),
        check_vma=False,
    )
```

time: 912 us -> 551 us (0.60)
  matrix products: 289 us -> 61.8 us
  other arithmetic: 133 us -> 38 us
  blocking collectives: 148 us -> 59.4 us
  starting transfers between devices: 13.1 us -> 57.5 us
  Pallas kernels: 0 us -> 30.5 us
  waiting for transfers between devices: 265 us -> 240 us
    dot_general x70 -> x24, matrix products: 289 us -> 61.8 us  [dot(): lax.dot_general(left, right, (((left_dim,), (right_dim,)), ((), ())), pre...]
    reduce_scatter x11 -> x0, waiting for transfers between devices: 183 us -> none  [the longest x1 35.9 us: local(): lax.psum_scatter(summed[8].astype(jnp.bfloat16), 'shard', scatter_dimensi...]
    ppermute x4 -> x40, waiting for transfers between devices: 33.5 us -> 173 us  [exchange(): lax.ppermute(x, axis, [(i, i ^ bit) for i in range(lax.axis_size(axis))])]
    all_gather x3 -> x6, waiting for transfers between devices: 0.02 us -> 66.6 us  [gathered(): return lax.all_gather(piece, 'shard', axis=0, tiled=True)]
    another operation x19 -> x16, other arithmetic: 62 us -> 4.42 us
    all_gather x10 -> x4, blocking collectives: 105 us -> 59.4 us  [the longest x2 35.1 us: gathered(): return lax.all_gather(piece, 'shard', axis=0, tiled=True)]
    ppermute x4 -> x40, starting transfers between devices: 11.9 us -> 57.3 us  [exchange(): lax.ppermute(x, axis, [(i, i ^ bit) for i in range(lax.axis_size(axis))])]
    reduce_sum x8 -> x1, other arithmetic: 34.3 us -> 0.16 us  [inverse_rms(): return lax.rsqrt(jnp.mean(source * source, -1, keepdims=True) + epsilon)]
  transfers between devices with their start and end apart: 21 -> 46, of which waited for: 15 -> 23; matrix products, arithmetic and copies ran while one was open for 18% -> 19% of each run, Pallas kernels for 0% -> 6%
where the time goes in v1:
time: 551 us; the launch traced here: 547 us
  waiting for transfers between devices  240 us (44%)
  matrix products  61.8 us (11%)
  blocking collectives  59.4 us (11%)
  starting transfers between devices  57.5 us (10%)
  local copies, waits for them, and re-layouts  43.3 us (8%)
  other arithmetic  38 us (7%)
  Pallas kernels  30.5 us (6%)
  between operations  15.9 us (3%)
    ppermute x40, waiting for transfers between devices, exchange(): lax.ppermute(x, axis, [(i, i ^ bit) for i in range(lax.axis_size(axis))])  173 us
    all_gather x6, waiting for transfers between devices, gathered(): return lax.all_gather(piece, 'shard', axis=0, tiled=True)  66.6 us
    dot_general x24, matrix products, dot(): lax.dot_general(left, right, (((left_dim,), (right_dim,)), ((), ())), pre...  61.8 us
    ppermute x40, starting transfers between devices, exchange(): lax.ppermute(x, axis, [(i, i ^ bit) for i in range(lax.axis_size(axis))])  57.3 us
    all_gather x2, blocking collectives, gathered(): return lax.all_gather(piece, 'shard', axis=0, tiled=True)  35.1 us
    all_gather x2, blocking collectives, forward_layer(): kv = lax.all_gather(jnp.concatenate([keys, values], 0), 'ctx', axis=0)  24.3 us
    pallas_call x2, Pallas kernels, attend_back(): pl.pallas_call(functools.partial(attend_back_kernel, blocks), out_shape=(...  19.7 us
    squeeze x24, local copies, waits for them, and re-layouts, reduce_rows(): send = lax.dynamic_index_in_dim(halves, 1 - mine, 1, keepdims=False)  13.9 us
  transfers between devices with their start and end apart: 46, of which 23 were waited for; matrix products, arithmetic and copies ran while one was open for 19% of the time, Pallas kernels for 6%

profile of v1, /device:TPU:0, one launch (start us, length us, event | category | flops | bytes accessed | tf_op | source)
XLA Modules:
  0.0 546.7 jit_solution(9864256084565389349)
XLA Ops:
  9.9 3.0 collective-permute-start
  12.9 3.8 collective-permute-done
  21.3 9.6 %collective-permute-done.2 = bf16[72,3072]{1,0:T(8,128)(2,1)S(1)} collective-permute-done((bf16[72,3072]{1,0:T(8,128)(2,1)S(1)}, bf16[72,3072]{1,0:T(8,128)(2,1)S(1)}, u32[]{:S(2)}, u32[]{:S(2)}) %collective-permute-start.2) | collective-permute-done | bytes 442400 | tf_op jit(solution)/shard_map/ppermute | solution.py:194
  33.6 4.8 collective-permute-done.3
  41.9 2.5 collective-permute-done.1
  44.5 18.7 %all_gather.39 = bf16[576,576]{1,0:T(8,128)(2,1)S(1)} all-gather(bf16[72,576]{1,0:T(8,128)(2,1)S(1)} %get-tuple-element.101), channel_id=1, replica_groups=mesh['section'=2,'ctx'=2,'shard'=8] {'shard'}, dimensions={0}, use_global_device_ids=true | all-gather | bytes 746496 | tf_op jit(solution)/shard_map/all_gather | solution.py:198
  63.2 16.4 %all_gather.45 = bf16[576,576]{1,0:T(8,128)(2,1)} all-gather(bf16[72,576]{1,0:T(8,128)(2,1)S(1)} %get-tuple-element.100), channel_id=1, replica_groups=mesh['section'=2,'ctx'=2,'shard'=8] {'shard'}, dimensions={0}, use_global_device_ids=true | all-gather | bytes 746496 | tf_op jit(solution)/shard_map/all_gather | solution.py:198
  83.8 12.3 %all-gather = bf16[768,512]{1,0:T(8,128)(2,1)S(1)} all-gather(bf16[384,512]{1,0:T(8,128)(2,1)S(1)} %pad_maximum_fusion.17), channel_id=2, replica_groups=mesh['section'=2,'ctx'=2,'shard'=8] {'ctx'}, dimensions={0}, use_global_device_ids=true | all-gather | bytes 1179648 | tf_op jit(solution)/shard_map/all_gather | solution.py:232
  96.4 5.3 shard_map.194
  104.0 9.1 %all-gather.11.cloned.1.call-done = bf16[576,3072]{1,0:T(8,128)(2,1)} async-done(((bf16[72,3072]{1,0:T(8,128)(2,1)}), bf16[576,3072]{1,0:T(8,128)(2,1)}) %all-gather.11.cloned.1.call-update) | async-done | bytes 3538960 | tf_op jit(solution)/shard_map/all_gather | solution.py:198
  113.2 4.7 fusion.79
  117.9 2.6 copy-done.4
  120.5 2.1 multiply_convert_fusion.5
  122.6 19.5 %all-gather.13.cloned.1.call-done = bf16[1536,576]{1,0:T(8,128)(2,1)} async-done(((bf16[192,576]{1,0:T(8,128)(2,1)}), bf16[1536,576]{1,0:T(8,128)(2,1)}) %all-gather.13.cloned.1.call-update) | async-done | bytes 1769488 | tf_op jit(solution)/shard_map/all_gather | solution.py:198
  142.2 3.3 fusion.25
  149.4 11.9 %all-gather.1 = bf16[768,512]{1,0:T(8,128)(2,1)S(1)} all-gather(bf16[384,512]{1,0:T(8,128)(2,1)S(1)} %pad_maximum_fusion.18), channel_id=3, replica_groups=mesh['section'=2,'ctx'=2,'shard'=8] {'ctx'}, dimensions={0}, use_global_device_ids=true | all-gather | bytes 1179648 | tf_op jit(solution)/shard_map/all_gather | solution.py:232
  161.4 5.5 %shard_map.195 = (bf16[576,512]{1,0:T(8,128)(2,1)S(1)}, f32[16,512]{1,0:T(8,128)S(1)}) custom-call(s32[1]{0:T(128)} %bitcast.1.pos_ref, bf16[576,512]{1,0:T(8,128)(2,1)S(1)} %bitcast.264, bf16[2,384,512]{2,1,0:T(8,128)(2,1)S(1)} %bitcast.260), custom_call_target="tpu_custom_call" | custom-call | flops 4831838208 | bytes 4194304 | tf_op jit(solution)/shard_map/pallas_call | solution.py:107
  168.6 16.7 %all-gather.17.cloned.1.call-done = bf16[576,3072]{1,0:T(8,128)(2,1)} async-done(((bf16[72,3072]{1,0:T(8,128)(2,1)}), bf16[576,3072]{1,0:T(8,128)(2,1)}) %all-gather.17.cloned.1.call-update) | async-done | bytes 3538960 | tf_op jit(solution)/shard_map/all_gather | solution.py:198
  185.3 7.8 %fusion.80 = f32[512,3072]{1,0:T(8,128)} fusion(bf16[576,3072]{1,0:T(8,128)(2,1)} %all-gather.17.cloned.1.call-done, f32[512,576]{0,1:T(8,128)} %get-tuple-element.110, f32[576]{0:T(1024)S(1)} %get-tuple-element.59, f32[512]{0:T(512)S(1)} %add_rsqrt_fusion), kind=kOutput, calls=%fused_computation.260 | convolution fusion | flops 1812824064 | bytes 11014400 | tf_op jit(solution)/shard_map/dot_general | solution.py:52
  193.1 21.2 %all-gather.19.cloned.1.call-done = bf16[1536,576]{1,0:T(8,128)(2,1)} async-done(((bf16[192,576]{1,0:T(8,128)(2,1)}), bf16[1536,576]{1,0:T(8,128)(2,1)}) %all-gather.19.cloned.1.call-update) | async-done | bytes 1769488 | tf_op jit(solution)/shard_map/all_gather | solution.py:198
  214.3 6.2 %multiply_convert_fusion.3 = (bf16[512,1536]{1,0:T(8,128)(2,1)S(1)}, bf16[512,1536]{1,0:T(8,128)(2,1)S(1)}, bf16[512,1536]{1,0:T(8,128)(2,1)S(1)}) fusion(f32[512,3072]{1,0:T(8,128)} %fusion.80, bf16[1536,576]{1,0:T(8,128)(2,1)} %all-gather.19.cloned.1.call-done, bf16[2,1,512,576]{2,3,1,0:T(8,128)(2,1)} %param.12, s32[]{:T(128)S(6)} %select_n.321), kind=kOutput, calls=%fused_computation.11 | convolution fusion | flops 918552576 | bytes 13565956 | tf_op jit(solution)/shard_map/dot_general | solution.py:52
  220.5 4.0 convolution_convert_fusion
  224.5 2.8 multiply_reduce_fusion
  230.6 2.3 convolution_convert_fusion.2
  232.9 3.9 copy.42
  236.8 2.3 dynamic-slice_bitcast_fusion.2
  239.4 9.9 %shard_map.196 = (f32[576,512]{1,0:T(8,128)S(1)}, f32[2,384,512]{2,1,0:T(8,128)S(1)}) custom-call(s32[1]{0:T(128)} %bitcast.1.pos_ref, bf16[576,512]{1,0:T(8,128)(2,1)S(1)} %bitcast.265, bf16[2,384,512]{2,1,0:T(8,128)(2,1)S(1)} %bitcast.261, f32[16,512]{1,0:T(8,128)S(1)} %get-tuple-element.21.log_ref, bf16[576,512]{1,0:T(8,128)(2,1)S(1)} %convolution_convert_fusion.9.dm_ref), custom_call_target="tpu_custom_call" | custom-call | flops 12079595520 | bytes 8388608 | tf_op jit(solution)/shard_map/pallas_call | solution.py:173
  251.3 10.8 %collective-permute-start.5 = (bf16[384,512]{1,0:T(8,128)(2,1)}, bf16[384,512]{1,0:T(8,128)(2,1)}, u32[]{:S(2)}, u32[]{:S(2)}) collective-permute-start(bf16[384,512]{1,0:T(8,128)(2,1)} %dynamic-slice_bitcast_fusion.11), channel_id=1, source_target_pairs={{0,8},{8,0},{1,9},{9,1},{2,10},{10,2},{3,11},{11,3},{4,12},{12,4},... | collective-permute-start | bytes 1179656 | tf_op jit(solution)/shard_map/ppermute | solution.py:194
  265.1 4.3 broadcast_select_fusion.2
  276.0 1.9 convolution_convert_fusion.4
  279.8 2.3 convolution_convert_fusion.3
  283.4 2.7 multiply_convert_fusion.1
  286.1 3.9 convolution_convert_fusion.1
  290.0 2.2 multiply_reduce_fusion.1
  294.7 3.9 copy.41
  298.6 2.2 dynamic-slice_bitcast_fusion.3
  300.9 2.8 dynamic-slice_bitcast_fusion.1
  307.5 9.7 %shard_map.197 = (f32[576,512]{1,0:T(8,128)S(1)}, f32[2,384,512]{2,1,0:T(8,128)S(1)}) custom-call(s32[1]{0:T(128)} %bitcast.1.pos_ref, bf16[576,512]{1,0:T(8,128)(2,1)S(1)} %bitcast.263, bf16[2,384,512]{2,1,0:T(8,128)(2,1)S(1)} %bitcast.259, f32[16,512]{1,0:T(8,128)S(1)} %get-tuple-element.24.log_ref, bf16[576,512]{1,0:T(8,128)(2,1)S(1)} %convolution_convert_fusion.8.dm_ref), custom_call_target="tpu_custom_call" | custom-call | flops 12079595520 | bytes 8388608 | tf_op jit(solution)/shard_map/pallas_call | solution.py:173
  325.4 10.1 %collective-permute-start.6 = (bf16[384,512]{1,0:T(8,128)(2,1)S(1)}, bf16[384,512]{1,0:T(8,128)(2,1)S(1)}, u32[]{:S(2)}, u32[]{:S(2)}) collective-permute-start(bf16[384,512]{1,0:T(8,128)(2,1)S(1)} %copy-done.54), channel_id=1, source_target_pairs={{0,8},{8,0},{1,9},{9,1},{2,10},{10,2},{3,11},{11,3},{4,12},{12,4},... | collective-permute-start | bytes 1179656 | tf_op jit(solution)/shard_map/ppermute | solution.py:194
  338.7 6.1 %collective-permute-done.6 = bf16[384,512]{1,0:T(8,128)(2,1)S(1)} collective-permute-done((bf16[384,512]{1,0:T(8,128)(2,1)S(1)}, bf16[384,512]{1,0:T(8,128)(2,1)S(1)}, u32[]{:S(2)}, u32[]{:S(2)}) %collective-permute-start.6) | collective-permute-done | bytes 393248 | tf_op jit(solution)/shard_map/ppermute | solution.py:194
  345.1 1.9 fusion.32
  347.0 1.9 convolution_convert_fusion.5
  353.9 4.9 collective-permute-done.17
  359.8 2.0 collective-permute-start.18
  363.2 4.9 collective-permute-done.21
  370.9 3.6 collective-permute-done.22
  374.6 1.8 collective-permute-start.23
  376.4 2.8 collective-permute-done.23
  382.6 11.0 %collective-permute-done.36 = bf16[2,192,576]{2,1,0:T(8,128)(2,1)S(1)} collective-permute-done((bf16[2,192,576]{2,1,0:T(8,128)(2,1)S(1)}, bf16[2,192,576]{2,1,0:T(8,128)(2,1)S(1)}, u32[]{:S(2)}, u32[]{:S(2)}) %collective-permute-start.36) | collective-permute-done | bytes 442400 | tf_op jit(solution)/shard_map/ppermute | solution.py:194
  394.5 1.8 collective-permute-start.33
  398.8 18.0 %collective-permute-done.9 = bf16[2,72,962]{2,1,0:T(8,128)(2,1)S(1)} collective-permute-done((bf16[2,72,962]{2,1,0:T(8,128)(2,1)S(1)}, bf16[2,72,962]{2,1,0:T(8,128)(2,1)S(1)}, u32[]{:S(2)}, u32[]{:S(2)}) %collective-permute-start.9) | collective-permute-done | bytes 277088 | tf_op jit(solution)/shard_map/ppermute | solution.py:194
  417.4 2.5 collective-permute-start.10
  420.7 20.4 %collective-permute-done.10 = bf16[1,72,962]{2,1,0:T(8,128)(2,1)S(1)} collective-permute-done((bf16[1,72,962]{2,1,0:T(8,128)(2,1)S(1)}, bf16[1,72,962]{2,1,0:T(8,128)(2,1)S(1)}, u32[]{:S(2)}, u32[]{:S(2)}) %collective-permute-start.10) | collective-permute-done | bytes 138560 | tf_op jit(solution)/shard_map/ppermute | solution.py:194
  441.7 2.3 fusion
  444.2 2.7 collective-permute-done.14
  447.0 1.8 collective-permute-start.15
  448.8 2.2 fusion.1
  451.1 15.6 %collective-permute-done.28 = bf16[2,72,3072]{2,1,0:T(8,128)(2,1)S(1)} collective-permute-done((bf16[2,72,3072]{2,1,0:T(8,128)(2,1)S(1)}, bf16[2,72,3072]{2,1,0:T(8,128)(2,1)S(1)}, u32[]{:S(2)}, u32[]{:S(2)}) %collective-permute-start.28) | collective-permute-done | bytes 884768 | tf_op jit(solution)/shard_map/ppermute | solution.py:194
  467.5 26.3 %collective-permute-done.25 = bf16[2,72,3072]{2,1,0:T(8,128)(2,1)S(1)} collective-permute-done((bf16[2,72,3072]{2,1,0:T(8,128)(2,1)S(1)}, bf16[2,72,3072]{2,1,0:T(8,128)(2,1)S(1)}, u32[]{:S(2)}, u32[]{:S(2)}) %collective-permute-start.25) | collective-permute-done | bytes 884768 | tf_op jit(solution)/shard_map/ppermute | solution.py:194
  496.7 18.0 %collective-permute-done.26 = bf16[1,72,3072]{2,1,0:T(8,128)(2,1)S(1)} collective-permute-done((bf16[1,72,3072]{2,1,0:T(8,128)(2,1)S(1)}, bf16[1,72,3072]{2,1,0:T(8,128)(2,1)S(1)}, u32[]{:S(2)}, u32[]{:S(2)}) %collective-permute-start.26) | collective-permute-done | bytes 442400 | tf_op jit(solution)/shard_map/ppermute | solution.py:194
  517.3 1.8 collective-permute-start.39
  519.1 7.9 %collective-permute-done.30 = bf16[72,3072]{1,0:T(8,128)(2,1)S(1)} collective-permute-done((bf16[72,3072]{1,0:T(8,128)(2,1)S(1)}, bf16[72,3072]{1,0:T(8,128)(2,1)S(1)}, u32[]{:S(2)}, u32[]{:S(2)}) %collective-permute-start.30) | collective-permute-done | bytes 442400 | tf_op jit(solution)/shard_map/ppermute | solution.py:194
  527.3 1.8 collective-permute-start.31
  530.7 7.9 %collective-permute-done.31 = bf16[72,3072]{1,0:T(8,128)(2,1)S(1)} collective-permute-done((bf16[72,3072]{1,0:T(8,128)(2,1)S(1)}, bf16[72,3072]{1,0:T(8,128)(2,1)S(1)}, u32[]{:S(2)}, u32[]{:S(2)}) %collective-permute-start.31) | collective-permute-done | bytes 442400 | tf_op jit(solution)/shard_map/ppermute | solution.py:194
  (351 shorter events, 89.7 us)
Async XLA Ops:
  7.2 23.7 %copy-start.49 = (bf16[1,72,1536]{2,1,0:T(8,128)(2,1)S(1)}, bf16[1,72,1536]{2,1,0:T(8,128)(2,1)}, u32[]{:S(2)}) copy-start(bf16[1,72,1536]{2,1,0:T(8,128)(2,1)} %param.19) | copy-start | bytes 663556
  7.2 23.7 %copy-start.48 = (bf16[1,72,1536]{2,1,0:T(8,128)(2,1)S(1)}, bf16[1,72,1536]{2,1,0:T(8,128)(2,1)}, u32[]{:S(2)}) copy-start(bf16[1,72,1536]{2,1,0:T(8,128)(2,1)} %param.20) | copy-start | bytes 663556
  7.2 72.5 %all-gather.9.cloned.1.call-start = ((), (), s32[]{:S(2)}) async-start(), calls=%async_computation | async-start | bytes 1327104 | tf_op jit(solution)/shard_map/all_gather | solution.py:198
  9.9 6.9 %collective-permute-start = (bf16[72,962]{1,0:T(8,128)(2,1)S(1)}, bf16[72,962]{1,0:T(8,128)(2,1)S(1)}, u32[]{:S(2)}, u32[]{:S(2)}) collective-permute-start(bf16[72,962]{1,0:T(8,128)(2,1)S(1)} %concatenate.44), channel_id=1, source_target_pairs={{0,16},{16,0},{1,17},{17,1},{2,18},{18,2},{3,19},{19,3},{4,20},{20... | collective-permute-start | bytes 415592 | tf_op jit(solution)/shard_map/ppermute | solution.py:194
  17.5 85.0 %all-gather.15.cloned.1.call-start = ((), (), s32[]{:S(2)}) async-start(), calls=%async_computation.3 | async-start | bytes 1327104 | tf_op jit(solution)/shard_map/all_gather | solution.py:198
  18.3 13.8 %copy-start.56 = (bf16[1,192,576]{2,1,0:T(8,128)(2,1)S(1)}, bf16[1,192,576]{2,1,0:T(8,128)(2,1)}, u32[]{:S(2)}) copy-start(bf16[1,192,576]{2,1,0:T(8,128)(2,1)} %param.21) | copy-start | bytes 663556
  18.3 94.9 %all-gather.11.cloned.1.call-start = ((), (), s32[]{:S(2)}) async-start(), calls=%async_computation.1 | async-start | bytes 3981312 | tf_op jit(solution)/shard_map/all_gather | solution.py:198
  19.5 20.4 %copy-start.58 = (bf16[1,72,576]{2,1,0:T(8,128)(2,1)S(1)}, bf16[1,72,576]{2,1,0:T(8,128)(2,1)}, u32[]{:S(2)}) copy-start(bf16[1,72,576]{2,1,0:T(8,128)(2,1)} %param.17) | copy-start | bytes 248836
  19.5 21.9 %copy-start.24 = (bf16[2,1,512,576]{2,3,1,0:T(8,128)(2,1)S(1)}, bf16[2,1,512,576]{2,3,1,0:T(8,128)(2,1)}, u32[]{:S(2)}) copy-start(bf16[2,1,512,576]{2,3,1,0:T(8,128)(2,1)} %param.11) | copy-start | bytes 3538948
  19.5 11.4 %collective-permute-start.2 = (bf16[72,3072]{1,0:T(8,128)(2,1)S(1)}, bf16[72,3072]{1,0:T(8,128)(2,1)S(1)}, u32[]{:S(2)}, u32[]{:S(2)}) collective-permute-start(bf16[72,3072]{1,0:T(8,128)(2,1)S(1)} %pad_maximum_fusion.12), channel_id=1, source_target_pairs={{0,16},{16,0},{1,17},{17,1},{2,18},{18,2},{3,19},{19,3},{4,20},{20... | collective-permute-start | bytes 1327112 | tf_op jit(solution)/shard_map/ppermute | solution.py:194
  32.0 110.1 %all-gather.13.cloned.1.call-start = ((), (), s32[]{:S(2)}) async-start(), calls=%async_computation.2 | async-start | bytes 2211840 | tf_op jit(solution)/shard_map/all_gather | solution.py:198
  32.1 6.3 %collective-permute-start.3 = (bf16[192,576]{1,0:T(8,128)(2,1)S(1)}, bf16[192,576]{1,0:T(8,128)(2,1)S(1)}, u32[]{:S(2)}, u32[]{:S(2)}) collective-permute-start(bf16[192,576]{1,0:T(8,128)(2,1)S(1)} %bitcast.316), channel_id=1, source_target_pairs={{0,16},{16,0},{1,17},{17,1},{2,18},{18,2},{3,19},{19,3},{4,20},{20... | collective-permute-start | bytes 663560 | tf_op jit(solution)/shard_map/ppermute | solution.py:194
  39.2 146.1 %all-gather.17.cloned.1.call-start = ((), (), s32[]{:S(2)}) async-start(), calls=%async_computation.4 | async-start | bytes 3981312 | tf_op jit(solution)/shard_map/all_gather | solution.py:198
  39.8 174.5 %all-gather.19.cloned.1.call-start = ((), (), s32[]{:S(2)}) async-start(), calls=%async_computation.5 | async-start | bytes 2211840 | tf_op jit(solution)/shard_map/all_gather | solution.py:198
  39.9 4.6 collective-permute-start.1
  41.8 54.3 %copy-start.41 = (f32[32,512]{1,0:T(8,128)}, f32[32,512]{1,0:T(8,128)S(1)}, u32[]{:S(2)}) copy-start(f32[32,512]{1,0:T(8,128)S(1)} %get-tuple-element.103) | copy-start | bytes 196612
  63.2 38.5 %copy-start.13 = (bf16[576,576]{1,0:T(8,128)(2,1)}, bf16[576,576]{1,0:T(8,128)(2,1)S(1)}, u32[]{:S(2)}) copy-start(bf16[576,576]{1,0:T(8,128)(2,1)S(1)} %all_gather.39) | copy-start | bytes 1990660
  83.6 12.5 %slice-start.2 = ((f32[960,512]{1,0:T(8,128)}), f32[576,512]{1,0:T(8,128)S(1)}, s32[]{:S(2)}) async-start(f32[960,512]{1,0:T(8,128)} %copy-done.22), calls=%async_computation.8 | async-start | bytes 2359296 | tf_op jit(solution)/shard_map/slice | solution.py:229
  102.4 39.7 %copy-start.7 = (f32[512,576]{0,1:T(8,128)}, f32[512,576]{0,1:T(8,128)S(1)}, u32[]{:S(2)}) copy-start(f32[512,576]{0,1:T(8,128)S(1)} %get-tuple-element.106) | copy-start | bytes 3538948
  104.0 41.4 %copy-start.64 = (f32[576]{0:T(1024)}, f32[576]{0:T(1024)S(1)}, u32[]{:S(2)}) copy-start(f32[576]{0:T(1024)S(1)} %get-tuple-element.60) | copy-start | bytes 6916
  145.4 21.5 %copy-start.17 = (bf16[512,576]{0,1:T(8,128)(2,1)}, bf16[512,576]{0,1:T(8,128)(2,1)S(1)}, u32[]{:S(2)}) copy-start(bf16[512,576]{0,1:T(8,128)(2,1)S(1)} %get-tuple-element.108) | copy-start | bytes 1769476
  149.4 17.5 %copy-start.2 = (bf16[9,2,32,512]{3,2,1,0:T(8,128)(2,1)}, bf16[9,2,32,512]{3,2,1,0:T(8,128)(2,1)S(1)}, u32[]{:S(2)}) copy-start(bf16[9,2,32,512]{3,2,1,0:T(8,128)(2,1)S(1)} %maximum_multiply_fusion.1) | copy-start | bytes 1769476
  239.1 112.2 %collective-permute-start.35 = (bf16[4,192,576]{2,1,0:T(8,128)(2,1)}, bf16[4,192,576]{2,1,0:T(8,128)(2,1)}, u32[]{:S(2)}, u32[]{:S(2)}) collective-permute-start(bf16[4,192,576]{2,1,0:T(8,128)(2,1)} %dynamic-slice_bitcast_fusion.2), channel_id=1, source_target_pairs={{0,1},{1,0},{2,3},{3,2},{4,5},{5,4},{6,7},{7,6},{8,9},{9,8},{10,11... | collective-permute-start | bytes 2654216 | tf_op jit(solution)/shard_map/ppermute | solution.py:194
  249.3 12.8 %copy-start.31 = (bf16[576,3072]{1,0:T(8,128)(2,1)S(1)}, bf16[576,3072]{1,0:T(8,128)(2,1)}, u32[]{:S(2)}) copy-start(bf16[576,3072]{1,0:T(8,128)(2,1)} %convolution_convert_fusion) | copy-start | bytes 10616836
  250.5 13.0 %copy-start.36 = (bf16[2,384,512]{2,1,0:T(8,128)(2,1)}, bf16[2,384,512]{2,1,0:T(8,128)(2,1)S(1)}, u32[]{:S(2)}) copy-start(bf16[2,384,512]{2,1,0:T(8,128)(2,1)S(1)} %convert_element_type.538) | copy-start | bytes 2359300
  251.3 23.3 %collective-permute-start.5 = (bf16[384,512]{1,0:T(8,128)(2,1)}, bf16[384,512]{1,0:T(8,128)(2,1)}, u32[]{:S(2)}, u32[]{:S(2)}) collective-permute-start(bf16[384,512]{1,0:T(8,128)(2,1)} %dynamic-slice_bitcast_fusion.11), channel_id=1, source_target_pairs={{0,8},{8,0},{1,9},{9,1},{2,10},{10,2},{3,11},{11,3},{4,12},{12,4},... | collective-permute-start | bytes 1179656 | tf_op jit(solution)/shard_map/ppermute | solution.py:194
  263.6 178.1 %collective-permute-start.27 = (bf16[4,72,3072]{2,1,0:T(8,128)(2,1)}, bf16[4,72,3072]{2,1,0:T(8,128)(2,1)}, u32[]{:S(2)}, u32[]{:S(2)}) collective-permute-start(bf16[4,72,3072]{2,1,0:T(8,128)(2,1)} %dynamic-slice_bitcast_fusion), channel_id=1, source_target_pairs={{0,1},{1,0},{2,3},{3,2},{4,5},{5,4},{6,7},{7,6},{8,9},{9,8},{10,11... | collective-permute-start | bytes 5308424 | tf_op jit(solution)/shard_map/ppermute | solution.py:194
  264.3 6.8 %collective-permute-start.19 = (bf16[4,72,576]{2,1,0:T(8,128)(2,1)}, bf16[4,72,576]{2,1,0:T(8,128)(2,1)}, u32[]{:S(2)}, u32[]{:S(2)}) collective-permute-start(bf16[4,72,576]{2,1,0:T(8,128)(2,1)} %dynamic-slice_bitcast_fusion.12), channel_id=1, source_target_pairs={{0,1},{1,0},{2,3},{3,2},{4,5},{5,4},{6,7},{7,6},{8,9},{9,8},{10,11... | collective-permute-start | bytes 995336 | tf_op jit(solution)/shard_map/ppermute | solution.py:194
  269.4 55.9 %collective-permute-start.4 = (bf16[512,576]{0,1:T(8,128)(2,1)}, bf16[512,576]{0,1:T(8,128)(2,1)}, u32[]{:S(2)}, u32[]{:S(2)}) collective-permute-start(bf16[512,576]{0,1:T(8,128)(2,1)} %get-tuple-element.111), channel_id=1, source_target_pairs={{0,16},{16,0},{1,17},{17,1},{2,18},{18,2},{3,19},{19,3},{4,20},{20... | collective-permute-start | bytes 1769480 | tf_op jit(solution)/shard_map/ppermute | solution.py:194
  273.1 49.9 %collective-permute-start.20 = (bf16[2,72,576]{2,1,0:T(8,128)(2,1)}, bf16[2,72,576]{2,1,0:T(8,128)(2,1)}, u32[]{:S(2)}, u32[]{:S(2)}) collective-permute-start(bf16[2,72,576]{2,1,0:T(8,128)(2,1)} %dynamic-slice_bitcast_fusion.16), channel_id=1, source_target_pairs={{0,2},{1,3},{2,0},{3,1},{4,6},{5,7},{6,4},{7,5},{8,10},{9,11},{10,... | collective-permute-start | bytes 497672 | tf_op jit(solution)/shard_map/ppermute | solution.py:194
  300.9 79.1 %collective-permute-start.32 = (bf16[4,192,576]{2,1,0:T(8,128)(2,1)}, bf16[4,192,576]{2,1,0:T(8,128)(2,1)}, u32[]{:S(2)}, u32[]{:S(2)}) collective-permute-start(bf16[4,192,576]{2,1,0:T(8,128)(2,1)} %dynamic-slice_bitcast_fusion.3), channel_id=1, source_target_pairs={{0,1},{1,0},{2,3},{3,2},{4,5},{5,4},{6,7},{7,6},{8,9},{9,8},{10,11... | collective-permute-start | bytes 2654216 | tf_op jit(solution)/shard_map/ppermute | solution.py:194
  320.1 15.4 %copy-start.20 = (bf16[512,576]{0,1:T(8,128)(2,1)S(1)}, bf16[512,576]{0,1:T(8,128)(2,1)}, u32[]{:S(2)}) copy-start(bf16[512,576]{0,1:T(8,128)(2,1)} %copy-done.17) | copy-start | bytes 1769476
  321.8 13.6 %copy-start.52 = (bf16[512,576]{0,1:T(8,128)(2,1)S(1)}, bf16[512,576]{0,1:T(8,128)(2,1)}, u32[]{:S(2)}) copy-start(bf16[512,576]{0,1:T(8,128)(2,1)} %get-tuple-element.112) | copy-start | bytes 1769476
  323.0 14.8 %collective-permute-start.16 = (bf16[4,72,576]{2,1,0:T(8,128)(2,1)}, bf16[4,72,576]{2,1,0:T(8,128)(2,1)S(1)}, u32[]{:S(2)}, u32[]{:S(2)}) collective-permute-start(bf16[4,72,576]{2,1,0:T(8,128)(2,1)} %dynamic-slice_bitcast_fusion.13), channel_id=1, source_target_pairs={{0,1},{1,0},{2,3},{3,2},{4,5},{5,4},{6,7},{7,6},{8,9},{9,8},{10,11... | collective-permute-start | bytes 995336 | tf_op jit(solution)/shard_map/ppermute | solution.py:194
  325.4 19.4 %collective-permute-start.6 = (bf16[384,512]{1,0:T(8,128)(2,1)S(1)}, bf16[384,512]{1,0:T(8,128)(2,1)S(1)}, u32[]{:S(2)}, u32[]{:S(2)}) collective-permute-start(bf16[384,512]{1,0:T(8,128)(2,1)S(1)} %copy-done.54), channel_id=1, source_target_pairs={{0,8},{8,0},{1,9},{9,1},{2,10},{10,2},{3,11},{11,3},{4,12},{12,4},... | collective-permute-start | bytes 1179656 | tf_op jit(solution)/shard_map/ppermute | solution.py:194
  337.8 111.0 %collective-permute-start.24 = (bf16[4,72,3072]{2,1,0:T(8,128)(2,1)}, bf16[4,72,3072]{2,1,0:T(8,128)(2,1)}, u32[]{:S(2)}, u32[]{:S(2)}) collective-permute-start(bf16[4,72,3072]{2,1,0:T(8,128)(2,1)} %dynamic-slice_bitcast_fusion.1), channel_id=1, source_target_pairs={{0,1},{1,0},{2,3},{3,2},{4,5},{5,4},{6,7},{7,6},{8,9},{9,8},{10,11... | collective-permute-start | bytes 5308424 | tf_op jit(solution)/shard_map/ppermute | solution.py:194
  344.8 15.1 %collective-permute-start.11 = (bf16[4,72,962]{2,1,0:T(8,128)(2,1)}, bf16[4,72,962]{2,1,0:T(8,128)(2,1)}, u32[]{:S(2)}, u32[]{:S(2)}) collective-permute-start(bf16[4,72,962]{2,1,0:T(8,128)(2,1)} %dynamic-slice_bitcast_fusion.6), channel_id=1, source_target_pairs={{0,1},{1,0},{2,3},{3,2},{4,5},{5,4},{6,7},{7,6},{8,9},{9,8},{10,11... | collective-permute-start | bytes 1662344 | tf_op jit(solution)/shard_map/ppermute | solution.py:194
  351.3 10.6 %copy-start.28 = (bf16[4,2,72,962]{3,2,0,1:T(8,128)(2,1)S(1)}, bf16[4,2,72,962]{3,2,0,1:T(8,128)(2,1)}, u32[]{:S(2)}) copy-start(bf16[4,2,72,962]{3,2,0,1:T(8,128)(2,1)} %copy-done.27) | copy-start | bytes 3324676
  351.8 7.0 %collective-permute-start.17 = (bf16[2,72,576]{2,1,0:T(8,128)(2,1)S(1)}, bf16[2,72,576]{2,1,0:T(8,128)(2,1)S(1)}, u32[]{:S(2)}, u32[]{:S(2)}) collective-permute-start(bf16[2,72,576]{2,1,0:T(8,128)(2,1)S(1)} %copy-done.57), channel_id=1, source_target_pairs={{0,2},{1,3},{2,0},{3,1},{4,6},{5,7},{6,4},{7,5},{8,10},{9,11},{10,... | collective-permute-start | bytes 497672 | tf_op jit(solution)/shard_map/ppermute | solution.py:194
  358.8 9.3 %collective-permute-start.21 = (bf16[1,72,576]{2,1,0:T(8,128)(2,1)S(1)}, bf16[1,72,576]{2,1,0:T(8,128)(2,1)S(1)}, u32[]{:S(2)}, u32[]{:S(2)}) collective-permute-start(bf16[1,72,576]{2,1,0:T(8,128)(2,1)S(1)} %copy-done.59), channel_id=1, source_target_pairs={{0,4},{1,5},{2,6},{3,7},{4,0},{5,1},{6,2},{7,3},{8,12},{9,13},{10,... | collective-permute-start | bytes 248840 | tf_op jit(solution)/shard_map/ppermute | solution.py:194
  359.8 10.0 %collective-permute-start.18 = (bf16[1,72,576]{2,1,0:T(8,128)(2,1)S(1)}, bf16[1,72,576]{2,1,0:T(8,128)(2,1)S(1)}, u32[]{:S(2)}, u32[]{:S(2)}) collective-permute-start(bf16[1,72,576]{2,1,0:T(8,128)(2,1)S(1)} %constant_dynamic-slice_fusion.5), channel_id=1, source_target_pairs={{0,4},{1,5},{2,6},{3,7},{4,0},{5,1},{6,2},{7,3},{8,12},{9,13},{10,... | collective-permute-start | bytes 248840 | tf_op jit(solution)/shard_map/ppermute | solution.py:194
  369.9 4.6 collective-permute-start.22
  370.8 9.1 %collective-permute-start.12 = (bf16[2,72,962]{2,1,0:T(8,128)(2,1)S(1)}, bf16[2,72,962]{2,1,0:T(8,128)(2,1)S(1)}, u32[]{:S(2)}, u32[]{:S(2)}) collective-permute-start(bf16[2,72,962]{2,1,0:T(8,128)(2,1)S(1)} %dynamic-slice_bitcast_fusion.14), channel_id=1, source_target_pairs={{0,2},{1,3},{2,0},{3,1},{4,6},{5,7},{6,4},{7,5},{8,10},{9,11},{10,... | collective-permute-start | bytes 831176 | tf_op jit(solution)/shard_map/ppermute | solution.py:194
  374.6 4.6 collective-permute-start.23
  379.2 15.3 %collective-permute-start.8 = (bf16[4,72,962]{2,1,0:T(8,128)(2,1)S(1)}, bf16[4,72,962]{2,1,0:T(8,128)(2,1)S(1)}, u32[]{:S(2)}, u32[]{:S(2)}) collective-permute-start(bf16[4,72,962]{2,1,0:T(8,128)(2,1)S(1)} %dynamic-slice_bitcast_fusion.7), channel_id=1, source_target_pairs={{0,1},{1,0},{2,3},{3,2},{4,5},{5,4},{6,7},{7,6},{8,9},{9,8},{10,11... | collective-permute-start | bytes 1662344 | tf_op jit(solution)/shard_map/ppermute | solution.py:194
  379.9 13.6 %collective-permute-start.36 = (bf16[2,192,576]{2,1,0:T(8,128)(2,1)S(1)}, bf16[2,192,576]{2,1,0:T(8,128)(2,1)S(1)}, u32[]{:S(2)}, u32[]{:S(2)}) collective-permute-start(bf16[2,192,576]{2,1,0:T(8,128)(2,1)S(1)} %dynamic-slice_bitcast_fusion.8), channel_id=1, source_target_pairs={{0,2},{1,3},{2,0},{3,1},{4,6},{5,7},{6,4},{7,5},{8,10},{9,11},{10,... | collective-permute-start | bytes 1327112 | tf_op jit(solution)/shard_map/ppermute | solution.py:194
  380.0 16.5 %collective-permute-start.7 = (bf16[512,576]{0,1:T(8,128)(2,1)S(1)}, bf16[512,576]{0,1:T(8,128)(2,1)S(1)}, u32[]{:S(2)}, u32[]{:S(2)}) collective-permute-start(bf16[512,576]{0,1:T(8,128)(2,1)S(1)} %get-tuple-element.63), channel_id=1, source_target_pairs={{0,16},{16,0},{1,17},{17,1},{2,18},{18,2},{3,19},{19,3},{4,20},{20... | collective-permute-start | bytes 1769480 | tf_op jit(solution)/shard_map/ppermute | solution.py:194
  393.5 26.6 %collective-permute-start.13 = (bf16[1,72,962]{2,1,0:T(8,128)(2,1)S(1)}, bf16[1,72,962]{2,1,0:T(8,128)(2,1)S(1)}, u32[]{:S(2)}, u32[]{:S(2)}) collective-permute-start(bf16[1,72,962]{2,1,0:T(8,128)(2,1)S(1)} %constant_dynamic-slice_fusion.6), channel_id=1, source_target_pairs={{0,4},{1,5},{2,6},{3,7},{4,0},{5,1},{6,2},{7,3},{8,12},{9,13},{10,... | collective-permute-start | bytes 415592 | tf_op jit(solution)/shard_map/ppermute | solution.py:194
  394.5 22.9 %collective-permute-start.33 = (bf16[2,192,576]{2,1,0:T(8,128)(2,1)S(1)}, bf16[2,192,576]{2,1,0:T(8,128)(2,1)S(1)}, u32[]{:S(2)}, u32[]{:S(2)}) collective-permute-start(bf16[2,192,576]{2,1,0:T(8,128)(2,1)S(1)} %dynamic-slice_bitcast_fusion.9), channel_id=1, source_target_pairs={{0,2},{1,3},{2,0},{3,1},{4,6},{5,7},{6,4},{7,5},{8,10},{9,11},{10,... | collective-permute-start | bytes 1327112 | tf_op jit(solution)/shard_map/ppermute | solution.py:194
  396.6 20.2 %collective-permute-start.9 = (bf16[2,72,962]{2,1,0:T(8,128)(2,1)S(1)}, bf16[2,72,962]{2,1,0:T(8,128)(2,1)S(1)}, u32[]{:S(2)}, u32[]{:S(2)}) collective-permute-start(bf16[2,72,962]{2,1,0:T(8,128)(2,1)S(1)} %dynamic-slice_bitcast_fusion.15), channel_id=1, source_target_pairs={{0,2},{1,3},{2,0},{3,1},{4,6},{5,7},{6,4},{7,5},{8,10},{9,11},{10,... | collective-permute-start | bytes 831176 | tf_op jit(solution)/shard_map/ppermute | solution.py:194
  416.8 77.4 %collective-permute-start.37 = (bf16[1,192,576]{2,1,0:T(8,128)(2,1)S(1)}, bf16[1,192,576]{2,1,0:T(8,128)(2,1)S(1)}, u32[]{:S(2)}, u32[]{:S(2)}) collective-permute-start(bf16[1,192,576]{2,1,0:T(8,128)(2,1)S(1)} %constant_dynamic-slice_fusion), channel_id=1, source_target_pairs={{0,4},{1,5},{2,6},{3,7},{4,0},{5,1},{6,2},{7,3},{8,12},{9,13},{10,... | collective-permute-start | bytes 663560 | tf_op jit(solution)/shard_map/ppermute | solution.py:194
  417.3 24.4 %copy-start.32 = (bf16[576,3072]{1,0:T(8,128)(2,1)S(1)}, bf16[576,3072]{1,0:T(8,128)(2,1)}, u32[]{:S(2)}) copy-start(bf16[576,3072]{1,0:T(8,128)(2,1)} %convolution_convert_fusion) | copy-start | bytes 10616836
  417.4 23.6 %collective-permute-start.10 = (bf16[1,72,962]{2,1,0:T(8,128)(2,1)S(1)}, bf16[1,72,962]{2,1,0:T(8,128)(2,1)S(1)}, u32[]{:S(2)}, u32[]{:S(2)}) collective-permute-start(bf16[1,72,962]{2,1,0:T(8,128)(2,1)S(1)} %constant_dynamic-slice_fusion.7), channel_id=1, source_target_pairs={{0,4},{1,5},{2,6},{3,7},{4,0},{5,1},{6,2},{7,3},{8,12},{9,13},{10,... | collective-permute-start | bytes 415592 | tf_op jit(solution)/shard_map/ppermute | solution.py:194
  420.1 74.1 %collective-permute-start.34 = (bf16[1,192,576]{2,1,0:T(8,128)(2,1)S(1)}, bf16[1,192,576]{2,1,0:T(8,128)(2,1)S(1)}, u32[]{:S(2)}, u32[]{:S(2)}) collective-permute-start(bf16[1,192,576]{2,1,0:T(8,128)(2,1)S(1)} %constant_dynamic-slice_fusion.1), channel_id=1, source_target_pairs={{0,4},{1,5},{2,6},{3,7},{4,0},{5,1},{6,2},{7,3},{8,12},{9,13},{10,... | collective-permute-start | bytes 663560 | tf_op jit(solution)/shard_map/ppermute | solution.py:194
  441.1 5.7 %collective-permute-start.14 = (bf16[72,962]{1,0:T(8,128)(2,1)S(1)}, bf16[72,962]{1,0:T(8,128)(2,1)S(1)}, u32[]{:S(2)}, u32[]{:S(2)}) collective-permute-start(bf16[72,962]{1,0:T(8,128)(2,1)S(1)} %select_bitcast_fusion.6), channel_id=1, source_target_pairs={{0,16},{16,0},{1,17},{17,1},{2,18},{18,2},{3,19},{19,3},{4,20},{20... | collective-permute-start | bytes 415592 | tf_op jit(solution)/shard_map/ppermute | solution.py:194
  444.1 22.6 %collective-permute-start.28 = (bf16[2,72,3072]{2,1,0:T(8,128)(2,1)S(1)}, bf16[2,72,3072]{2,1,0:T(8,128)(2,1)S(1)}, u32[]{:S(2)}, u32[]{:S(2)}) collective-permute-start(bf16[2,72,3072]{2,1,0:T(8,128)(2,1)S(1)} %dynamic-slice_bitcast_fusion.4), channel_id=1, source_target_pairs={{0,2},{1,3},{2,0},{3,1},{4,6},{5,7},{6,4},{7,5},{8,10},{9,11},{10,... | collective-permute-start | bytes 2654216 | tf_op jit(solution)/shard_map/ppermute | solution.py:194
  447.0 48.9 %collective-permute-start.15 = (bf16[72,962]{1,0:T(8,128)(2,1)S(1)}, bf16[72,962]{1,0:T(8,128)(2,1)S(1)}, u32[]{:S(2)}, u32[]{:S(2)}) collective-permute-start(bf16[72,962]{1,0:T(8,128)(2,1)S(1)} %fusion.60), channel_id=1, source_target_pairs={{0,8},{8,0},{1,9},{9,1},{2,10},{10,2},{3,11},{11,3},{4,12},{12,4},... | collective-permute-start | bytes 415592 | tf_op jit(solution)/shard_map/ppermute | solution.py:194
  451.0 42.7 %collective-permute-start.25 = (bf16[2,72,3072]{2,1,0:T(8,128)(2,1)S(1)}, bf16[2,72,3072]{2,1,0:T(8,128)(2,1)S(1)}, u32[]{:S(2)}, u32[]{:S(2)}) collective-permute-start(bf16[2,72,3072]{2,1,0:T(8,128)(2,1)S(1)} %dynamic-slice_bitcast_fusion.5), channel_id=1, source_target_pairs={{0,2},{1,3},{2,0},{3,1},{4,6},{5,7},{6,4},{7,5},{8,10},{9,11},{10,... | collective-permute-start | bytes 2654216 | tf_op jit(solution)/shard_map/ppermute | solution.py:194
  467.0 29.7 %collective-permute-start.29 = (bf16[1,72,3072]{2,1,0:T(8,128)(2,1)S(1)}, bf16[1,72,3072]{2,1,0:T(8,128)(2,1)S(1)}, u32[]{:S(2)}, u32[]{:S(2)}) collective-permute-start(bf16[1,72,3072]{2,1,0:T(8,128)(2,1)S(1)} %constant_dynamic-slice_fusion.2), channel_id=1, source_target_pairs={{0,4},{1,5},{2,6},{3,7},{4,0},{5,1},{6,2},{7,3},{8,12},{9,13},{10,... | collective-permute-start | bytes 1327112 | tf_op jit(solution)/shard_map/ppermute | solution.py:194
  494.1 20.6 %collective-permute-start.26 = (bf16[1,72,3072]{2,1,0:T(8,128)(2,1)S(1)}, bf16[1,72,3072]{2,1,0:T(8,128)(2,1)S(1)}, u32[]{:S(2)}, u32[]{:S(2)}) collective-permute-start(bf16[1,72,3072]{2,1,0:T(8,128)(2,1)S(1)} %constant_dynamic-slice_fusion.3), channel_id=1, source_target_pairs={{0,4},{1,5},{2,6},{3,7},{4,0},{5,1},{6,2},{7,3},{8,12},{9,13},{10,... | collective-permute-start | bytes 1327112 | tf_op jit(solution)/shard_map/ppermute | solution.py:194
  494.3 22.8 %collective-permute-start.38 = (bf16[192,576]{1,0:T(8,128)(2,1)S(1)}, bf16[192,576]{1,0:T(8,128)(2,1)S(1)}, u32[]{:S(2)}, u32[]{:S(2)}) collective-permute-start(bf16[192,576]{1,0:T(8,128)(2,1)S(1)} %select_bitcast_fusion.5), channel_id=1, source_target_pairs={{0,16},{16,0},{1,17},{17,1},{2,18},{18,2},{3,19},{19,3},{4,20},{20... | collective-permute-start | bytes 663560 | tf_op jit(solution)/shard_map/ppermute | solution.py:194
  514.8 12.2 %collective-permute-start.30 = (bf16[72,3072]{1,0:T(8,128)(2,1)S(1)}, bf16[72,3072]{1,0:T(8,128)(2,1)S(1)}, u32[]{:S(2)}, u32[]{:S(2)}) collective-permute-start(bf16[72,3072]{1,0:T(8,128)(2,1)S(1)} %select_bitcast_fusion.4), channel_id=1, source_target_pairs={{0,16},{16,0},{1,17},{17,1},{2,18},{18,2},{3,19},{19,3},{4,20},{20... | collective-permute-start | bytes 1327112 | tf_op jit(solution)/shard_map/ppermute | solution.py:194
  517.3 12.5 %collective-permute-start.39 = (bf16[192,576]{1,0:T(8,128)(2,1)S(1)}, bf16[192,576]{1,0:T(8,128)(2,1)S(1)}, u32[]{:S(2)}, u32[]{:S(2)}) collective-permute-start(bf16[192,576]{1,0:T(8,128)(2,1)S(1)} %fusion.55), channel_id=1, source_target_pairs={{0,8},{8,0},{1,9},{9,1},{2,10},{10,2},{3,11},{11,3},{4,12},{12,4},... | collective-permute-start | bytes 663560 | tf_op jit(solution)/shard_map/ppermute | solution.py:194
  527.3 11.3 %collective-permute-start.31 = (bf16[72,3072]{1,0:T(8,128)(2,1)S(1)}, bf16[72,3072]{1,0:T(8,128)(2,1)S(1)}, u32[]{:S(2)}, u32[]{:S(2)}) collective-permute-start(bf16[72,3072]{1,0:T(8,128)(2,1)S(1)} %fusion.47), channel_id=1, source_target_pairs={{0,8},{8,0},{1,9},{9,1},{2,10},{10,2},{3,11},{11,3},{4,12},{12,4},... | collective-permute-start | bytes 1327112 | tf_op jit(solution)/shard_map/ppermute | solution.py:194
  (57 other events, 194.0 us)
Sparse Core Ops, SparseCore 0:
  17.6 24.1 all-gather.8
  44.0 26.0 all-gather.14
  72.4 40.7 all-gather.10
  115.2 26.8 all-gather.12
  144.2 41.0 all-gather.16
  187.3 26.8 all-gather.18
